TPU v7x, 32 devices: a whole 2x2x4 slice. The times are simulated.
32 devices in a mesh: groups: 2 (over y), wide: 4 (over z), narrow: 4 (over x, core).
Axes of the slice: x: 2, y: 2, z: 4, core: 2. Of those that a mesh axis runs over, the one named last changes fastest.
Arguments:
- activations: bfloat16 [2048, 8192], P(('groups', 'wide'), 'narrow'), parts along dimension 0, may hold values from -6 to 6
- request_tenants: int32 [2048, 1], P(('groups', 'wide')), parts along dimension 0, may hold values from 0 to 63; in each aligned block of 256 rows (0 to 255, 256 to 511, ...) at most 16 rows name the same one
- adapter_slot: int32 [64], replicated, may hold values from 0 to 63, each once
- shared_weight: bfloat16 [8192, 2048], P(None, 'narrow'), may hold values from -0.0625 to 0.0625
- adapter_down_weight: bfloat16 [64, 8192, 128], P('wide', 'narrow'), may hold values from -0.0625 to 0.0625
- adapter_up_weight: bfloat16 [64, 64, 2048], P('wide', None, 'narrow'), may hold values from -0.75 to 0.75
Outputs:
- projected: bfloat16 [2048, 2048], P(('groups', 'wide'), 'narrow'), parts along dimension 0
There are 2 independent parts, one for each index of `groups`. A program takes and returns all parts, laid end to end along the dimension named above; an argument that names none is the same for every part. Nothing has to cross between parts.
Inputs may be any that keep to these rules, and one draw needn't show every extreme that they name: `request_tenants`: in each aligned block of 256 rows (the rows of one device) no tenant is named by more than 16 rows, a bound that some block reaches; every tenant is named by some row. `adapter_slot`: A permutation of the tenants.
All inputs are finite; a program needn't handle non-finite values.
Results may differ from a plain program's by a relative error of at most 0.007.
Values may be sent and summed in bfloat16 or wider, within the bound.
No kernel may reach another device: no remote copies, remote signals or barrier semaphores. Data moves between devices by JAX's collectives and lax.ppermute only.
A program may use at most 128 MiB of HBM per device.

v0:
```python
import jax
import jax.numpy as jnp
from jax import lax
from jax.sharding import PartitionSpec as P

KEY_VALUE_COLS = 1024
ADAPTER_RANK = 64
MOST = 16


def on_device(
    activations,
    request_tenants,
    adapter_slot,
    shared_weight,
    adapter_down_weight,
    adapter_up_weight,
):
    row_count = activations.shape[0]
    feature_count = activations.shape[1]
    col_count = shared_weight.shape[1]
    tenant_count = adapter_slot.shape[0]
    local_row_count = adapter_down_weight.shape[0]
    wide_size = lax.axis_size("wide")
    tenant = request_tenants[:, 0]
    onehot = (tenant[:, None] == jnp.arange(tenant_count, dtype=jnp.int32)[None, :]).astype(
        jnp.int32
    )
    slot_row = jnp.sum(onehot * adapter_slot[None, :], axis=1)
    before = jnp.cumsum(onehot, axis=0) - onehot
    position = jnp.sum(onehot * before, axis=1)
    target = slot_row * MOST + position
    outgoing = (
        jnp.zeros((tenant_count * MOST, feature_count), activations.dtype)
        .at[target]
        .set(activations)
    )
    outgoing = outgoing.reshape(wide_size, local_row_count, MOST, feature_count)
    column_index = lax.axis_index("narrow") * col_count + jnp.arange(col_count, dtype=jnp.int32)
    key_column_mask = (column_index < KEY_VALUE_COLS).astype(adapter_up_weight.dtype)
    value_column_mask = (column_index >= KEY_VALUE_COLS).astype(adapter_up_weight.dtype)
    partial_value = jnp.einsum(
        "wlmd,ldr->wlmr",
        lax.all_to_all(outgoing, "wide", split_axis=0, concat_axis=0, tiled=True),
        adapter_down_weight,
        preferred_element_type=jnp.float32,
    )
    returned = lax.all_to_all(partial_value, "wide", split_axis=0, concat_axis=0, tiled=True)
    base_out = jnp.dot(
        lax.all_gather(activations, "narrow", axis=1, tiled=True),
        shared_weight,
        preferred_element_type=jnp.float32,
    )
    own_rows = returned.reshape(tenant_count * MOST, returned.shape[-1])[target]
    reduced_rank_output = lax.psum(own_rows, "narrow").astype(jnp.bfloat16)
    key_rank = reduced_rank_output[:, :ADAPTER_RANK]
    value_rank = reduced_rank_output[:, ADAPTER_RANK:]
    device_portion = lax.all_gather(adapter_up_weight, "wide", axis=0, tiled=True)
    piece_count = device_portion.shape[0]
    slot_ids = jnp.arange(piece_count, dtype=jnp.int32)
    select = (slot_row[:, None] == slot_ids[None, :]).astype(jnp.bfloat16)
    left_key = (select[:, :, None] * key_rank[:, None, :]).reshape(
        row_count, piece_count * ADAPTER_RANK
    )
    left_value = (select[:, :, None] * value_rank[:, None, :]).reshape(
        row_count, piece_count * ADAPTER_RANK
    )
    flattened = device_portion.reshape(piece_count * ADAPTER_RANK, col_count)
    running = jnp.dot(left_key, flattened * key_column_mask, preferred_element_type=jnp.float32)
    summed = running + jnp.dot(
        left_value, flattened * value_column_mask, preferred_element_type=jnp.float32
    )
    correction = summed.astype(jnp.bfloat16)
    return (base_out + correction.astype(jnp.float32)).astype(jnp.bfloat16)


def solution(mesh):
    in_specs = (
        P(("groups", "wide"), "narrow"),
        P(("groups", "wide"), None),
        P(),
        P(None, "narrow"),
        P("wide", "narrow", None),
        P("wide", None, "narrow"),
    )
    out_specs = P(("groups", "wide"), "narrow")
    return jax.shard_map(
        on_device, mesh=mesh, in_specs=in_specs, out_specs=out_specs, check_vma=False
    )
```

profile of v0, /device:TPU:0, one launch (start us, length us, event | category | flops | bytes accessed | tf_op | source)
XLA Modules:
  0.0 239.7 jit_solution(15678579464767165665)
XLA Ops:
  6.5 0.0 all-gather.5.cloned.1.call-start
  6.5 0.7 all-gather.5.cloned.1.call-update
  7.3 0.7 fusion.52
  7.9 0.6 reduce-window.6
  8.6 0.2 slice_reduce_fusion
  8.8 0.8 select_reduce_fusion
  9.6 5.5 %scatter_custom_fusion = bf16[1024,2048]{1,0:T(8,128)(2,1)} fusion(s32[256]{0:T(256)S(1)} %bitcast.50, bf16[256,2048]{1,0:T(8,128)(2,1)} %param.6, bf16[]{:T(256)} %constant.7.clone.1), kind=kCustom, calls=%fused_computation.13 | custom fusion | bytes 4194816 | tf_op jit(solution)/shard_map/scatter | solution.py:36
  15.1 6.3 %all-to-all-start = ((bf16[4,16,16,2048]{3,2,1,0:T(8,128)(2,1)}), bf16[4,16,16,2048]{3,2,1,0:T(8,128)(2,1)}, u32[]{:S(2)}, u32[]{:S(2)}) async-start(bf16[4,16,16,2048]{3,2,1,0:T(8,128)(2,1)} %bitcast.46), calls=%async_computation | async-start | bytes 8388608 | tf_op jit(solution)/shard_map/all_to_all | solution.py:44
  21.4 0.7 all-gather.3.cloned.1.call-update
  22.2 159.4 %all-to-all-done = bf16[4,16,16,2048]{3,2,1,0:T(8,128)(2,1)} async-done(((bf16[4,16,16,2048]{3,2,1,0:T(8,128)(2,1)}), bf16[4,16,16,2048]{3,2,1,0:T(8,128)(2,1)}, u32[]{:S(2)}, u32[]{:S(2)}) %all-to-all-start) | async-done | bytes 4194336 | tf_op jit(solution)/shard_map/all_to_all | solution.py:44
  181.6 6.3 %fusion.23 = f32[4,16,16,128]{3,2,0,1:T(8,128)S(1)} fusion(bf16[16,2048,128]{2,1,0:T(8,128)(2,1)} %param.10, bf16[4,16,16,2048]{3,2,1,0:T(8,128)(2,1)} %all-to-all-done), kind=kOutput, calls=%fused_computation.17 | convolution fusion | flops 536870912 | bytes 13107200 | tf_op jit(solution)/shard_map/wlmd,ldr->wlmr/dot_general | solution.py:42
  187.9 0.9 copy.16
  188.8 3.5 %all-to-all-start.1 = ((f32[4,16,16,128]{3,2,1,0:T(8,128)}), f32[4,16,16,128]{3,2,1,0:T(8,128)S(1)}, u32[]{:S(2)}, u32[]{:S(2)}) async-start(f32[4,16,16,128]{3,2,1,0:T(8,128)} %copy.16), calls=%async_computation.1 | async-start | bytes 1048576 | tf_op jit(solution)/shard_map/all_to_all | solution.py:48
  192.3 14.9 %all-to-all-done.1 = f32[4,16,16,128]{3,2,1,0:T(8,128)S(1)} async-done(((f32[4,16,16,128]{3,2,1,0:T(8,128)}), f32[4,16,16,128]{3,2,1,0:T(8,128)S(1)}, u32[]{:S(2)}, u32[]{:S(2)}) %all-to-all-start.1) | async-done | bytes 524320 | tf_op jit(solution)/shard_map/all_to_all | solution.py:48
  207.3 0.7 gather_fusion
  208.0 11.8 %all-reduce.1 = bf16[256,128]{1,0:T(8,128)(2,1)S(1)} all-reduce(f32[256,128]{1,0:T(8,128)S(1)} %gather_fusion), channel_id=1, replica_groups=mesh['groups'=2,'wide'=4,'narrow'=4] {'narrow'}, use_global_device_ids=true, to_apply=%region_5.6 | all-reduce | flops 32768 | bytes 196608 | tf_op jit(solution)/shard_map/psum | solution.py:55
  219.9 0.1 fusion.57
  220.0 0.1 copy.17
  220.0 0.1 copy.18
  220.1 0.0 all-gather.5.cloned.1.call-done
  220.2 3.6 %fusion.13 = f32[256,512]{1,0:T(8,128)S(1)} fusion(bf16[64,64,512]{2,1,0:T(8,128)(2,1)} %all-gather.5.cloned.1.call-done, bf16[512]{0:T(512)(128)(2,1)S(1)} %fusion.55, bf16[256,64]{0,1:T(8,128)(2,1)S(1)} %copy.17, bf16[256,64]{0,1:T(8,128)(2,1)S(1)} %fusion.51), kind=kOutput, calls=%fused_computation.15 | convolution fusion | flops 1076887552 | bytes 4785152 | tf_op jit(solution)/shard_map/dot_general | solution.py:69
  223.8 1.3 fusion.39
  225.1 0.0 all-gather.3.cloned.1.call-done
  225.1 7.7 %fusion.33 = bf16[256,512]{1,0:T(8,128)(2,1)} fusion(f32[256,512]{1,0:T(8,128)S(1)} %fusion.39, bf16[256,8192]{1,0:T(8,128)(2,1)} %all-gather.3.cloned.1.call-done, bf16[8192,512]{1,0:T(8,128)(2,1)} %param.9), kind=kOutput, calls=%fused_computation.20 | convolution fusion | flops 2147745792 | bytes 13369344 | tf_op jit(solution)/shard_map/dot_general | solution.py:49
  (11 shorter events, 0.1 us)
Async XLA Ops:
  6.5 213.6 %all-gather.5.cloned.1.call-start = ((), (), s32[]{:S(2)}) async-start(), calls=%async_computation.3 | async-start | bytes 5242880 | tf_op jit(solution)/shard_map/all_gather | solution.py:58
  15.1 166.5 %all-to-all-start = ((bf16[4,16,16,2048]{3,2,1,0:T(8,128)(2,1)}), bf16[4,16,16,2048]{3,2,1,0:T(8,128)(2,1)}, u32[]{:S(2)}, u32[]{:S(2)}) async-start(bf16[4,16,16,2048]{3,2,1,0:T(8,128)(2,1)} %bitcast.46), calls=%async_computation | async-start | bytes 8388608 | tf_op jit(solution)/shard_map/all_to_all | solution.py:44
  21.4 203.7 %all-gather.3.cloned.1.call-start = ((), (), s32[]{:S(2)}) async-start(), calls=%async_computation.2 | async-start | bytes 5242880 | tf_op jit(solution)/shard_map/all_gather | solution.py:50
  188.8 18.5 %all-to-all-start.1 = ((f32[4,16,16,128]{3,2,1,0:T(8,128)}), f32[4,16,16,128]{3,2,1,0:T(8,128)S(1)}, u32[]{:S(2)}, u32[]{:S(2)}) async-start(f32[4,16,16,128]{3,2,1,0:T(8,128)} %copy.16), calls=%async_computation.1 | async-start | bytes 1048576 | tf_op jit(solution)/shard_map/all_to_all | solution.py:48
  220.2 3.6 %copy-start = (bf16[64,64,512]{2,1,0:T(8,128)(2,1)S(1)}, bf16[64,64,512]{2,1,0:T(8,128)(2,1)}, u32[]{:S(2)}) copy-start(bf16[64,64,512]{2,1,0:T(8,128)(2,1)} %all-gather.5.cloned.1.call-done) | copy-start | bytes 12582916
Sparse Core Ops, SparseCore 0:
  8.9 161.6 all-gather.4
  172.1 32.6 all-gather.2
where the time goes:
time: 240 us
  waiting for transfers between devices  176 us (73%)
  matrix products  18.9 us (8%)
  between operations  13.5 us (6%)
  blocking collectives  11.8 us (5%)
  starting transfers between devices  9.79 us (4%)
  local copies, waits for them, and re-layouts  7.6 us (3%)
    all_to_all x1, waiting for transfers between devices, on_device(): lax.all_to_all(outgoing, 'wide', split_axis=0, concat_axis=0, tiled=True)  159 us
    all_to_all x1, waiting for transfers between devices, on_device(): lax.all_to_all(partial_value, 'wide', split_axis=0, concat_axis=0, tiled=...  14.9 us
    psum x1, blocking collectives, on_device(): reduced_rank_output = lax.psum(own_rows, 'narrow').astype(jnp.bfloat16)  11.8 us
    dot_general x1, matrix products, on_device(): jnp.dot(lax.all_gather(activations, 'narrow', axis=1, tiled=True), shared...  7.69 us
    dot_general x1, matrix products, on_device(): jnp.einsum('wlmd,ldr->wlmr', lax.all_to_all(outgoing, 'wide', split_axis=...  6.33 us
    all_to_all x1, starting transfers between devices, on_device(): lax.all_to_all(outgoing, 'wide', split_axis=0, concat_axis=0, tiled=True)  6.32 us
    scatter x1, local copies, waits for them, and re-layouts, on_device(): outgoing = jnp.zeros((tenant_count * MOST, feature_count), activations.dt...  5.51 us
  transfers between devices with their start and end apart: 4, of which 2 were waited for; matrix products, arithmetic and copies ran while one was open for 9% of the time, Pallas kernels for 0%

commit v1 on v0

v1 whole, which is shorter than its diff:
```python
import functools

import jax
import jax.numpy as jnp
from jax import lax
from jax.experimental import pallas as pl
from jax.experimental.pallas import tpu as pltpu
from jax.sharding import PartitionSpec as P

KEY_VALUE_COLS = 1024
LANES = 128
MOST = 16
NEAR = 2
NEAR_ROWS = 112
FAR_ROWS = 96
VMEM = pltpu.VMEM
MIB = 1 << 20

f32, bf16, i32 = jnp.float32, jnp.bfloat16, jnp.int32


def block_rows(k, local_count):
    most = -(-(local_count * MOST + 1) // 32) * 32
    return min(NEAR_ROWS if k < NEAR else FAR_ROWS, most)


def swap(x, axis, k):
    size = lax.axis_size(axis)
    return lax.ppermute(x, axis, [(i, i ^ k) for i in range(size)])


def params(mib):
    return pltpu.CompilerParams(vmem_limit_bytes=mib * MIB)


def pack_kernel(local_count, where_ref, tenant_ref, slot_ref, act_ref, place_ref, *rest):
    blocks, perms = rest[: len(rest) // 2], rest[len(rest) // 2 :]
    wide_size = len(blocks)
    rows = tenant_ref.shape[1]

    @pl.when(pl.program_id(0) == 0)
    def _():
        tenants = slot_ref.shape[1]
        tenant = tenant_ref[...]
        named = tenant == lax.broadcasted_iota(i32, (tenants, rows), 0)
        slots = jnp.broadcast_to(slot_ref[...].astype(f32), (8, tenants)).astype(bf16)
        slot = jnp.dot(slots, named.astype(f32).astype(bf16), preferred_element_type=f32)[:1]
        dest = jnp.floor((slot + 0.5) * (1.0 / local_count))
        adapter = slot - dest * local_count + 1.0
        leap = jnp.bitwise_xor(dest.astype(i32), where_ref[0])
        padded = max(8, wide_size)
        goes = leap == lax.broadcasted_iota(i32, (padded, rows), 0)
        goes_f = goes.astype(f32)
        earlier = lax.broadcasted_iota(i32, (rows, rows), 0) < lax.broadcasted_iota(
            i32, (rows, rows), 1
        )
        before = jnp.dot(
            goes_f.astype(bf16), earlier.astype(f32).astype(bf16), preferred_element_type=f32
        )
        position = jnp.sum(goes_f * before, axis=0, keepdims=True).astype(i32)
        adapters = jnp.broadcast_to(adapter, (8, rows)).astype(bf16)
        place = jnp.full((1, rows), -1, i32)
        more = jnp.zeros((1, rows), i32)
        offset = 0
        here = []
        for k in range(wide_size):
            held = block_rows(k, local_count) - 1
            mine = position - where_ref[1] * held
            mine = jnp.where(leap == k, mine, -1)
            more = jnp.maximum(more, jnp.where(mine >= held, 1, 0))
            mine = jnp.where(mine < held, mine, -1)
            place = jnp.where(mine >= 0, mine + offset, place)
            offset += held + 1
            here.append(mine)
        any_more = jnp.max(more.astype(f32), axis=1, keepdims=True)
        for k in range(wide_size):
            count = block_rows(k, local_count)
            perm = (lax.broadcasted_iota(i32, (count, rows), 0) == here[k]).astype(f32).astype(bf16)
            perms[k][...] = perm
            filler = jnp.zeros((LANES - count, rows), bf16)
            ids = lax.dot_general(
                adapters,
                jnp.concatenate([perm, filler], axis=0),
                (((1,), (1,)), ((), ())),
                preferred_element_type=f32,
            )[:1]
            lane = lax.broadcasted_iota(i32, (1, LANES), 1)
            ids = jnp.where(lane == LANES - 1, any_more, ids)
            last = lax.broadcasted_iota(i32, (count, LANES), 0) == count - 1
            body = jnp.dot(perm, act_ref[:, :LANES], preferred_element_type=f32)
            blocks[k][:, :LANES] = jnp.where(last, ids, body).astype(bf16)
            blocks[k][:, LANES:] = jnp.dot(
                perm, act_ref[:, LANES:], preferred_element_type=f32
            ).astype(bf16)
        place_ref[...] = jnp.broadcast_to(place.astype(f32), (LANES, rows)).T

    @pl.when(pl.program_id(0) > 0)
    def _():
        for k in range(wide_size):
            blocks[k][...] = jnp.dot(perms[k][...], act_ref[...], preferred_element_type=f32).astype(
                bf16
            )


def pack(where, tenant, slot, activations, wide_size, local_count):
    rows, features = activations.shape
    chunk = min(512, features)
    counts = [block_rows(k, local_count) for k in range(wide_size)]
    return pl.pallas_call(
        functools.partial(pack_kernel, local_count),
        grid=(features // chunk,),
        out_shape=[jax.ShapeDtypeStruct((rows, LANES), f32)]
        + [jax.ShapeDtypeStruct((c, features), bf16) for c in counts],
        in_specs=[
            pl.BlockSpec(memory_space=pltpu.SMEM),
            pl.BlockSpec((1, rows), lambda i: (0, 0)),
            pl.BlockSpec((1, slot.shape[1]), lambda i: (0, 0)),
            pl.BlockSpec((rows, chunk), lambda i: (0, i)),
        ],
        out_specs=[pl.BlockSpec((rows, LANES), lambda i: (0, 0))]
        + [pl.BlockSpec((c, chunk), lambda i: (0, i)) for c in counts],
        scratch_shapes=[VMEM((c, rows), bf16) for c in counts],
        compiler_params=params(24),
        cost_estimate=pl.CostEstimate(
            flops=2 * sum(counts) * rows * features,
            bytes_accessed=2 * features * (rows + sum(counts)),
            transcendentals=0,
        ),
        name="pack_rows",
    )(where, tenant, slot, activations)


def down_kernel(count, cols, narrow_size, where_ref, *refs):
    xs, weight_ref = refs[:count], refs[count]
    ids_ref, flag_ref = refs[count + 1 : count + 3]
    parts = refs[count + 3 : count + 3 + narrow_size]
    held_ref, total_ref = refs[count + 3 + narrow_size :]
    step = pl.program_id(0)
    per_step = weight_ref.shape[0]

    @pl.when(step == 0)
    def _():
        offset = 0
        flag = jnp.zeros((8, LANES), f32)
        for x in xs:
            rows = x.shape[0]
            held_ref[pl.ds(offset, rows), :] = x[...]
            last = x[pl.ds(rows - 16, 16), :LANES].astype(f32)[15:]
            square = jnp.broadcast_to(last, (LANES, LANES))
            flag = jnp.maximum(flag, square[:8])
            turned = square.T[:rows]
            keep = lax.broadcasted_iota(i32, (rows, LANES), 0) < rows - 1
            ids_ref[pl.ds(offset, rows), :] = jnp.where(keep, turned, 0.0)
            offset += rows
        flag_ref[...] = flag
        total_ref[...] = jnp.zeros_like(total_ref)

    weights = jnp.concatenate([weight_ref[j] for j in range(per_step)], axis=1)
    found = jnp.dot(held_ref[...], weights, preferred_element_type=f32)
    ids = ids_ref[...]
    total = total_ref[...]
    for j in range(per_step):
        name = (step * per_step + j + 1).astype(f32)
        total = jnp.where(ids == name, found[:, j * LANES : (j + 1) * LANES], total)
    total_ref[...] = total

    @pl.when(step == pl.num_programs(0) - 1)
    def _():
        full = total_ref[...]
        half = full.shape[0] // 2
        rank = LANES // 2
        top, bottom = full[:half], full[half:]
        low = lax.broadcasted_iota(i32, (half, LANES), 1) < rank
        keys = jnp.where(low, top, pltpu.roll(bottom, rank, 1))
        values = jnp.where(low, pltpu.roll(top, rank, 1), bottom)
        for j in range(narrow_size):
            start = jnp.bitwise_xor(where_ref[2], j) * cols
            parts[j][...] = jnp.where(start >= KEY_VALUE_COLS, values, keys).astype(parts[j].dtype)


def down(where, blocks, weight, cols, narrow_size):
    adapters, features, width = weight.shape
    rows = sum(b.shape[0] for b in blocks)
    per_step = 2 if adapters % 2 == 0 else 1
    return pl.pallas_call(
        functools.partial(down_kernel, len(blocks), cols, narrow_size),
        grid=(adapters // per_step,),
        out_shape=[
            jax.ShapeDtypeStruct((rows, LANES), f32),
            jax.ShapeDtypeStruct((8, LANES), f32),
        ]
        + [jax.ShapeDtypeStruct((rows // 2, LANES), bf16 if j else f32) for j in range(narrow_size)],
        in_specs=[pl.BlockSpec(memory_space=pltpu.SMEM)]
        + [pl.BlockSpec(b.shape, lambda i: (0, 0)) for b in blocks]
        + [pl.BlockSpec((per_step, features, width), lambda i: (i, 0, 0))],
        out_specs=[
            pl.BlockSpec((rows, LANES), lambda i: (0, 0)),
            pl.BlockSpec((8, LANES), lambda i: (0, 0)),
        ]
        + [pl.BlockSpec((rows // 2, LANES), lambda i: (0, 0)) for _ in range(narrow_size)],
        scratch_shapes=[VMEM((rows, features), bf16), VMEM((rows, LANES), f32)],
        compiler_params=params(32),
        cost_estimate=pl.CostEstimate(
            flops=2 * rows * features * adapters * width,
            bytes_accessed=2 * features * (rows + adapters * width),
            transcendentals=0,
        ),
        name="down_maps",
    )(where, *blocks, weight)


def up_kernel(narrow_size, ids_ref, *refs):
    parts, weight_ref, outs = refs[:narrow_size], refs[narrow_size], refs[narrow_size + 1 :]
    total = parts[0][...]
    for part in parts[1:]:
        total = total + part[...].astype(f32)
    low_rank = total.astype(bf16).astype(f32)
    rank = LANES // 2
    turned = pltpu.roll(low_rank, rank, 1)
    low = lax.broadcasted_iota(i32, low_rank.shape, 1) < rank
    twice = jnp.concatenate(
        [jnp.where(low, low_rank, turned), jnp.where(low, turned, low_rank)], axis=0
    )
    ids = ids_ref[...]
    second = (lax.broadcasted_iota(i32, ids.shape, 1) >= rank).astype(f32)
    adapters = weight_ref.shape[0] // rank
    left = [
        jnp.where(ids - second == 2.0 * pair + 1.0, twice, 0.0).astype(bf16)
        for pair in range(adapters // 2)
    ]
    found = jnp.dot(jnp.concatenate(left, axis=1), weight_ref[...], preferred_element_type=f32)
    offset = 0
    for out in outs:
        rows = out.shape[0]
        out[...] = found[offset : offset + rows].astype(bf16)
        offset += rows


def up(ids, parts, weight, counts):
    cols = weight.shape[1]
    return pl.pallas_call(
        functools.partial(up_kernel, len(parts)),
        out_shape=[jax.ShapeDtypeStruct((c, cols), bf16) for c in counts],
        compiler_params=params(24),
        cost_estimate=pl.CostEstimate(
            flops=2 * sum(counts) * weight.size,
            bytes_accessed=2 * weight.size + 2 * sum(counts) * (cols + 512),
            transcendentals=0,
        ),
        name="up_maps",
    )(ids, *parts, weight)


def base_kernel(count, where_ref, *refs):
    acts, weight_ref, out_ref = refs[:count], refs[count], refs[count + 1]
    step = pl.program_id(0)
    for j in range(count):

        @pl.when(step == j)
        def _(j=j):
            found = jnp.dot(acts[j][...], weight_ref[...], preferred_element_type=f32)
            out_ref[...] = found if j == 0 else out_ref[...] + found


def base(where, acts, weight):
    rows, features = acts[0].shape
    cols = weight.shape[1]
    count = len(acts)
    return pl.pallas_call(
        functools.partial(base_kernel, count),
        grid_spec=pltpu.PrefetchScalarGridSpec(
            num_scalar_prefetch=1,
            grid=(count,),
            in_specs=[pl.BlockSpec((rows, features), lambda i, where: (0, 0)) for _ in acts]
            + [
                pl.BlockSpec(
                    (features, cols), lambda i, where: (jnp.bitwise_xor(where[2], i), 0)
                )
            ],
            out_specs=pl.BlockSpec((rows, cols), lambda i, where: (0, 0)),
        ),
        out_shape=jax.ShapeDtypeStruct((rows, cols), f32),
        compiler_params=params(24),
        cost_estimate=pl.CostEstimate(
            flops=2 * rows * weight.size,
            bytes_accessed=2 * weight.size + 2 * rows * features * count,
            transcendentals=0,
        ),
        name="shared_projection",
    )(where, *acts, weight)


def join_kernel(base_ref, place_ref, *refs):
    corrections, out_ref = refs[:-1], refs[-1]
    stacked = jnp.concatenate([c[...] for c in corrections], axis=0)
    rows, count = base_ref.shape[0], stacked.shape[0]
    place = place_ref[:, :1].astype(i32)
    perm = (lax.broadcasted_iota(i32, (rows, count), 1) == place).astype(f32).astype(bf16)
    found = jnp.dot(perm, stacked, preferred_element_type=f32)
    out_ref[...] = (base_ref[...] + found).astype(out_ref.dtype)


def join(base_out, place, corrections, dtype):
    rows, cols = base_out.shape
    count = sum(c.shape[0] for c in corrections)
    return pl.pallas_call(
        join_kernel,
        out_shape=jax.ShapeDtypeStruct((rows, cols), dtype),
        compiler_params=params(24),
        cost_estimate=pl.CostEstimate(
            flops=2 * rows * cols * count,
            bytes_accessed=2 * cols * (count + 3 * rows),
            transcendentals=0,
        ),
        name="join_corrections",
    )(base_out, place, *corrections)


def corrections_of(turn, axes, tenant, slot, activations, down_weight, up_weight):
    wide_size, narrow_size = lax.axis_size("wide"), lax.axis_size("narrow")
    cols = up_weight.shape[1]
    where = jnp.stack([axes[0], turn, axes[1]])
    place, *sent = pack(
        where, tenant, slot, activations, wide_size, down_weight.shape[0]
    )
    near = list(range(min(NEAR, wide_size)))
    far = list(range(NEAR, wide_size))
    got = {k: swap(sent[k], "wide", k) if k else sent[k] for k in reversed(range(wide_size))}
    answers = {}
    flags = []
    for group in (near, far):
        if not group:
            continue
        ids, flag, *parts = down(where, [got[k] for k in group], down_weight, cols, narrow_size)
        flags.append(flag[0, LANES - 1])
        parts = [swap(p, "narrow", j) if j else p for j, p in enumerate(parts)]
        outs = up(ids, parts, up_weight, [sent[k].shape[0] for k in group])
        for k, out in zip(group, outs):
            answers[k] = swap(out, "wide", k) if k else out
    more = functools.reduce(jnp.maximum, flags)
    return place, [answers[k] for k in range(wide_size)], more


def on_device(
    activations,
    request_tenants,
    adapter_slot,
    shared_weight,
    adapter_down_weight,
    adapter_up_weight,
):
    rows = activations.shape[0]
    narrow_size = lax.axis_size("narrow")
    axes = (lax.axis_index("wide").astype(i32), lax.axis_index("narrow").astype(i32))
    tenant = request_tenants.reshape(1, rows)
    slot = adapter_slot.reshape(1, -1)
    up_weight = adapter_up_weight.reshape(-1, adapter_up_weight.shape[-1])

    acts = [activations]
    bit = narrow_size // 2
    spread = {0: activations}
    while bit:
        spread.update({j ^ bit: swap(x, "narrow", bit) for j, x in list(spread.items())})
        bit //= 2
    acts = [spread[j] for j in range(narrow_size)]

    rest = (tenant, slot, activations, adapter_down_weight, up_weight)
    place, answers, more = corrections_of(jnp.int32(0), axes, *rest)
    base_out = base(jnp.stack([axes[0], axes[0], axes[1]]), acts, shared_weight)

    def one_turn(base_out):
        return join(base_out, place, answers, bf16)

    def all_turns(base_out):
        def turn_of(state):
            turn, _, total = state
            place, answers, more = corrections_of(turn, axes, *rest)
            return turn + 1, more, join(total, place, answers, f32)

        state = (jnp.int32(0), jnp.float32(1), base_out)
        return lax.while_loop(lambda s: s[1] > 0, turn_of, state)[2].astype(bf16)

    return lax.cond(more > 0, all_turns, one_turn, base_out)


def solution(mesh):
    in_specs = (
        P(("groups", "wide"), "narrow"),
        P(("groups", "wide"), None),
        P(),
        P(None, "narrow"),
        P("wide", "narrow", None),
        P("wide", None, "narrow"),
    )
    out_specs = P(("groups", "wide"), "narrow")
    return jax.shard_map(
        on_device, mesh=mesh, in_specs=in_specs, out_specs=out_specs, check_vma=False
    )
```

time: 240 us -> 107 us (0.45)
  waiting for transfers between devices: 176 us -> 51 us
  Pallas kernels: 0 us -> 28.7 us
  matrix products: 18.9 us -> 0 us
  starting transfers between devices: 9.79 us -> 22.9 us
  between operations: 13.5 us -> 1.32 us
  blocking collectives: 11.8 us -> 0 us
  local copies, waits for them, and re-layouts: 7.6 us -> 1.92 us
    all_to_all x2 -> x0, waiting for transfers between devices: 174 us -> none  [the longest x1 159 us: on_device(): lax.all_to_all(outgoing, 'wide', split_axis=0, concat_axis=0, tiled=True)]
    ppermute x0 -> x15, waiting for transfers between devices: none -> 51 us  [swap(): return lax.ppermute(x, axis, [(i, i ^ k) for i in range(size)])]
    pallas_call x0 -> x7, Pallas kernels: none -> 28.7 us  [the longest x2 15 us: down(): pl.pallas_call(functools.partial(down_kernel, len(blocks), cols, narrow_s...]
    ppermute x0 -> x15, starting transfers between devices: none -> 22.9 us  [swap(): return lax.ppermute(x, axis, [(i, i ^ k) for i in range(size)])]
    dot_general x4 -> x0, matrix products: 18.9 us -> none  [the longest x1 7.69 us: on_device(): jnp.dot(lax.all_gather(activations, 'narrow', axis=1, tiled=True), shared...]
    psum x1 -> x0, blocking collectives: 11.8 us -> none  [on_device(): reduced_rank_output = lax.psum(own_rows, 'narrow').astype(jnp.bfloat16)]
    all_to_all x2 -> x0, starting transfers between devices: 9.79 us -> none  [the longest x1 6.32 us: on_device(): lax.all_to_all(outgoing, 'wide', split_axis=0, concat_axis=0, tiled=True)]
    scatter x1 -> x0, local copies, waits for them, and re-layouts: 5.51 us -> none  [on_device(): outgoing = jnp.zeros((tenant_count * MOST, feature_count), activations.dt...]
  transfers between devices with their start and end apart: 4 -> 15, of which waited for: 2 -> 3; matrix products, arithmetic and copies ran while one was open for 9% -> 1% of each run, Pallas kernels for 0% -> 26%
where the time goes in v1:
time: 107 us; the launch traced here: 106 us
  waiting for transfers between devices  51 us (48%)
  Pallas kernels  28.7 us (27%)
  starting transfers between devices  22.9 us (21%)
  local copies, waits for them, and re-layouts  1.92 us (2%)
  between operations  1.32 us (1%)
    ppermute x15, waiting for transfers between devices, swap(): return lax.ppermute(x, axis, [(i, i ^ k) for i in range(size)])  51 us
    ppermute x15, starting transfers between devices, swap(): return lax.ppermute(x, axis, [(i, i ^ k) for i in range(size)])  22.9 us
    pallas_call x2, Pallas kernels, down(): pl.pallas_call(functools.partial(down_kernel, len(blocks), cols, narrow_s...  15 us
    pallas_call x1, Pallas kernels, base(): pl.pallas_call(functools.partial(base_kernel, count), grid_spec=pltpu.Pre...  5.55 us
    pallas_call x1, Pallas kernels, pack(): pl.pallas_call(functools.partial(pack_kernel, local_count), grid=(feature...  3.46 us
    pallas_call x2, Pallas kernels, up(): pl.pallas_call(functools.partial(up_kernel, len(parts)), out_shape=[jax.S...  3.3 us
  transfers between devices with their start and end apart: 15, of which 3 were waited for; matrix products, arithmetic and copies ran while one was open for 1% of the time, Pallas kernels for 26%

profile of v1, /device:TPU:0, one launch (start us, length us, event | category | flops | bytes accessed | tf_op | source)
XLA Modules:
  0.0 106.0 jit_solution(18155975812458927877)
XLA Ops:
  0.0 2.9 %collective-permute-start.16 = (bf16[256,2048]{1,0:T(8,128)(2,1)}, bf16[256,2048]{1,0:T(8,128)(2,1)S(1)}, u32[]{:S(2)}, u32[]{:S(2)}) collective-permute-start(bf16[256,2048]{1,0:T(8,128)(2,1)} %refs_0_.1), channel_id=1, source_target_pairs={{0,2},{1,3},{2,0},{3,1},{4,6},{5,7},{6,4},{7,5},{8,10},{9,11},{10,... | collective-permute-start | bytes 3145736 | tf_op jit(solution)/shard_map/ppermute | solution.py:29
  2.9 23.4 %collective-permute-done.16.refs_2_ = bf16[256,2048]{1,0:T(8,128)(2,1)S(1)} collective-permute-done((bf16[256,2048]{1,0:T(8,128)(2,1)}, bf16[256,2048]{1,0:T(8,128)(2,1)S(1)}, u32[]{:S(2)}, u32[]{:S(2)}) %collective-permute-start.16) | collective-permute-done | bytes 1048608 | tf_op jit(solution)/shard_map/ppermute | solution.py:29
  26.4 3.5 %pack_rows.2 = (f32[256,128]{1,0:T(8,128)S(1)}, bf16[112,2048]{1,0:T(8,128)(2,1)S(1)}, bf16[112,2048]{1,0:T(8,128)(2,1)S(1)}, bf16[96,2048]{1,0:T(8,128)(2,1)S(1)}, bf16[96,2048]{1,0:T(8,128)(2,1)S(1)}) custom-call(s32[3]{0:T(128)S(1)} %add_add_fusion.where_ref, s32[1,256]{1,0:T(1,128)} %bitcast.20, s32[1,64]{1,0:T(1,128)} %bitcast.22, bf16[256,2048]{1,0:T(8,128)(2,1)} %refs_0_.1), custom_call_target="tpu_custom_call" | custom-call | flops 436207616 | bytes 2752512 | tf_op jit(solution)/shard_map/pack_rows/pallas_call | solution.py:109
  29.9 2.9 %collective-permute-start.13 = (bf16[96,2048]{1,0:T(8,128)(2,1)S(1)}, bf16[96,2048]{1,0:T(8,128)(2,1)S(1)}, u32[]{:S(2)}, u32[]{:S(2)}) collective-permute-start(bf16[96,2048]{1,0:T(8,128)(2,1)S(1)} %get-tuple-element.146), channel_id=1, source_target_pairs={{0,8},{4,12},{8,0},{12,4},{1,9},{5,13},{9,1},{13,5},{2,10},{6,14},... | collective-permute-start | bytes 1179656 | tf_op jit(solution)/shard_map/ppermute | solution.py:29
  32.8 1.3 %collective-permute-start.14 = (bf16[96,2048]{1,0:T(8,128)(2,1)S(1)}, bf16[96,2048]{1,0:T(8,128)(2,1)S(1)}, u32[]{:S(2)}, u32[]{:S(2)}) collective-permute-start(bf16[96,2048]{1,0:T(8,128)(2,1)S(1)} %get-tuple-element.147), channel_id=1, source_target_pairs={{0,12},{4,8},{8,4},{12,0},{1,13},{5,9},{9,5},{13,1},{2,14},{6,10},... | collective-permute-start | bytes 1179656 | tf_op jit(solution)/shard_map/ppermute | solution.py:29
  34.1 0.2 collective-permute-start.12
  34.3 25.4 %collective-permute-done.13.refs_0_ = bf16[96,2048]{1,0:T(8,128)(2,1)S(1)} collective-permute-done((bf16[96,2048]{1,0:T(8,128)(2,1)S(1)}, bf16[96,2048]{1,0:T(8,128)(2,1)S(1)}, u32[]{:S(2)}, u32[]{:S(2)}) %collective-permute-start.13) | collective-permute-done | bytes 393248 | tf_op jit(solution)/shard_map/ppermute | solution.py:29
  59.7 7.3 %down_maps.5 = (f32[192,128]{1,0:T(8,128)S(1)}, f32[8,128]{1,0:T(8,128)S(1)}, f32[96,128]{1,0:T(8,128)S(1)}, bf16[96,128]{1,0:T(8,128)(2,1)S(1)}, bf16[96,128]{1...) custom-call(s32[3]{0:T(128)S(1)} %add_add_fusion.where_ref, bf16[96,2048]{1,0:T(8,128)(2,1)S(1)} %collective-permute-done.13.refs_0_, ...), custom_call_target="tpu_custom_call" | custom-call | flops 1610612736 | bytes 9175040 | tf_op jit(solution)/shard_map/down_maps/pallas_call | solution.py:185
  67.1 1.7 %collective-permute-start.23 = (bf16[96,128]{1,0:T(8,128)(2,1)S(1)}, bf16[96,128]{1,0:T(8,128)(2,1)S(1)}, u32[]{:S(2)}, u32[]{:S(2)}) collective-permute-start(bf16[96,128]{1,0:T(8,128)(2,1)S(1)} %get-tuple-element.160), channel_id=1, source_target_pairs={{0,2},{1,3},{2,0},{3,1},{4,6},{5,7},{6,4},{7,5},{8,10},{9,11},{10,... | collective-permute-start | bytes 73736 | tf_op jit(solution)/shard_map/ppermute | solution.py:29
  69.0 7.6 %down_maps.4 = (f32[224,128]{1,0:T(8,128)S(1)}, f32[8,128]{1,0:T(8,128)S(1)}, f32[112,128]{1,0:T(8,128)S(1)}, bf16[112,128]{1,0:T(8,128)(2,1)S(1)}, bf16[112,128...) custom-call(s32[3]{0:T(128)S(1)} %add_add_fusion.where_ref, bf16[112,2048]{1,0:T(8,128)(2,1)S(1)} %get-tuple-element.143.refs_0_, ...), custom_call_target="tpu_custom_call" | custom-call | flops 1879048192 | bytes 9306112 | tf_op jit(solution)/shard_map/down_maps/pallas_call | solution.py:185
  76.7 0.4 collective-permute-start.18
  77.1 1.7 %collective-permute-start.19 = (bf16[112,128]{1,0:T(8,128)(2,1)S(1)}, bf16[112,128]{1,0:T(8,128)(2,1)S(1)}, u32[]{:S(2)}, u32[]{:S(2)}) collective-permute-start(bf16[112,128]{1,0:T(8,128)(2,1)S(1)} %get-tuple-element.153), channel_id=1, source_target_pairs={{0,2},{1,3},{2,0},{3,1},{4,6},{5,7},{6,4},{7,5},{8,10},{9,11},{10,... | collective-permute-start | bytes 86024 | tf_op jit(solution)/shard_map/ppermute | solution.py:29
  78.8 0.6 slice.13
  79.4 1.6 %up_maps.5 = (bf16[96,512]{1,0:T(8,128)(2,1)S(1)}, bf16[96,512]{1,0:T(8,128)(2,1)S(1)}) custom-call(f32[192,128]{1,0:T(8,128)S(1)} %get-tuple-element.157.ids_ref, f32[96,128]{1,0:T(8,128)S(1)} %get-tuple-element.158.refs_0_, bf16[96,128]{1,0:T(8,128)(2,1)S(1)} %collective-permute-done.22.refs_1_, bf16[96,128]{1,0:T(8,128)(2,1)S(1)} %collective-permute-done.23.refs_2_, ...), custom_call_target="tpu_custom_call" | custom-call | flops 201326592 | bytes 1441792 | tf_op jit(solution)/shard_map/up_maps/pallas_call | solution.py:241
  81.0 0.6 slice.12
  82.9 10.7 %collective-permute-start.25 = (bf16[96,512]{1,0:T(8,128)(2,1)S(1)}, bf16[96,512]{1,0:T(8,128)(2,1)S(1)}, u32[]{:S(2)}, u32[]{:S(2)}) collective-permute-start(bf16[96,512]{1,0:T(8,128)(2,1)S(1)} %get-tuple-element.162), channel_id=1, source_target_pairs={{0,8},{4,12},{8,0},{12,4},{1,9},{5,13},{9,1},{13,5},{2,10},{6,14},... | collective-permute-start | bytes 294920 | tf_op jit(solution)/shard_map/ppermute | solution.py:29
  93.6 0.5 collective-permute-start.26
  94.1 1.7 %up_maps.4 = (bf16[112,512]{1,0:T(8,128)(2,1)S(1)}, bf16[112,512]{1,0:T(8,128)(2,1)S(1)}) custom-call(f32[224,128]{1,0:T(8,128)S(1)} %get-tuple-element.150.ids_ref, f32[112,128]{1,0:T(8,128)S(1)} %get-tuple-element.151.refs_0_, bf16[112,128]{1,0:T(8,128)(2,1)S(1)} %collective-permute-done.18.refs_1_, bf16[112,128]{1,0:T(8,128)(2,1)S(1)} %collective-permute-done.19.refs_2_, ...), custom_call_target="tpu_custom_call" | custom-call | flops 234881024 | bytes 1507328 | tf_op jit(solution)/shard_map/up_maps/pallas_call | solution.py:241
  95.8 0.2 collective-permute-start.21
  96.0 5.6 %shared_projection.1 = f32[256,512]{1,0:T(8,128)} custom-call(s32[3]{0:T(128)S(1)} %add_add_fusion.1.where_ref, bf16[256,2048]{1,0:T(8,128)(2,1)} %refs_0_.1, bf16[256,2048]{1,0:T(8,128)(2,1)S(1)} %collective-permute-done.15.refs_1_, bf16[256,2048]{1,0:T(8,128)(2,1)S(1)} %collective-permute-done.16.refs_2_, ...), custom_call_target="tpu_custom_call" | custom-call | flops 2147483648 | bytes 12582912 | tf_op jit(solution)/shard_map/shared_projection/pallas_call | solution.py:269
  101.6 2.2 %collective-permute-done.21 = bf16[112,512]{1,0:T(8,128)(2,1)S(1)} collective-permute-done((bf16[112,512]{1,0:T(8,128)(2,1)S(1)}, bf16[112,512]{1,0:T(8,128)(2,1)S(1)}, u32[]{:S(2)}, u32[]{:S(2)}) %collective-permute-start.21) | collective-permute-done | bytes 114720 | tf_op jit(solution)/shard_map/ppermute | solution.py:29
  103.8 1.4 %conditional.1 = (bf16[256,512]{1,0:T(8,128)(2,1)S(1)}) conditional(s32[]{:T(128)} %bitcast.8, (f32[256,512]{1,0:T(8,128)}, f32[256,128]{1,0:T(8,128)S(1)}, bf16[112,512]{1,0:T(8,128)(2,1)S(1)}, bf16[112,512]{1,0:T(8,128)(2,1)S(1)}, bf16[96,512]{1,0:T(8,128)(2,1)S(1)}, /*index=5*/bf16[96,512]{1,0:T(8,128)(2,1)S(1)}) %tuple.15, (s32[]{:T(128)}, ...), branch_computations={%region_0.0_spmd, %region_1.0_spmd} | conditional | flops 4471259136 | bytes 34095856 | solution.py:383
  103.8 1.4 %join_corrections.2 = bf16[256,512]{1,0:T(8,128)(2,1)S(1)} custom-call(f32[256,512]{1,0:T(8,128)} %get-tuple-element.76.base_ref, f32[256,128]{1,0:T(8,128)S(1)} %get-tuple-element.77.place_ref, bf16[112,512]{1,0:T(8,128)(2,1)S(1)} %get-tuple-element.78.refs_0_, bf16[112,512]{1,0:T(8,128)(2,1)S(1)} %get-tuple-element.79.refs_1_, ...), custom_call_target="tpu_custom_call" | custom-call | flops 109051904 | bytes 1212416 | tf_op jit(solution)/shard_map/cond/branch_0_fun/join_corrections/pallas_call | solution.py:306
  105.3 0.7 copy-done
  (29 shorter events, 0.4 us)
Async XLA Ops:
  0.0 26.3 %collective-permute-start.16 = (bf16[256,2048]{1,0:T(8,128)(2,1)}, bf16[256,2048]{1,0:T(8,128)(2,1)S(1)}, u32[]{:S(2)}, u32[]{:S(2)}) collective-permute-start(bf16[256,2048]{1,0:T(8,128)(2,1)} %refs_0_.1), channel_id=1, source_target_pairs={{0,2},{1,3},{2,0},{3,1},{4,6},{5,7},{6,4},{7,5},{8,10},{9,11},{10,... | collective-permute-start | bytes 3145736 | tf_op jit(solution)/shard_map/ppermute | solution.py:29
  2.9 93.1 %collective-permute-start.15 = (bf16[256,2048]{1,0:T(8,128)(2,1)}, bf16[256,2048]{1,0:T(8,128)(2,1)S(1)}, u32[]{:S(2)}, u32[]{:S(2)}) collective-permute-start(bf16[256,2048]{1,0:T(8,128)(2,1)} %refs_0_.1), channel_id=1, source_target_pairs={{0,1},{1,0},{2,3},{3,2},{4,5},{5,4},{6,7},{7,6},{8,9},{9,8},{10,11... | collective-permute-start | bytes 3145736 | tf_op jit(solution)/shard_map/ppermute | solution.py:29
  26.3 69.7 %collective-permute-start.17 = (bf16[256,2048]{1,0:T(8,128)(2,1)S(1)}, bf16[256,2048]{1,0:T(8,128)(2,1)S(1)}, u32[]{:S(2)}, u32[]{:S(2)}) collective-permute-start(bf16[256,2048]{1,0:T(8,128)(2,1)S(1)} %collective-permute-done.16.refs_2_), channel_id=1, source_target_pairs={{0,1},{1,0},{2,3},{3,2},{4,5},{5,4},{6,7},{7,6},{8,9},{9,8},{10,11... | collective-permute-start | bytes 3145736 | tf_op jit(solution)/shard_map/ppermute | solution.py:29
  29.9 29.9 %collective-permute-start.13 = (bf16[96,2048]{1,0:T(8,128)(2,1)S(1)}, bf16[96,2048]{1,0:T(8,128)(2,1)S(1)}, u32[]{:S(2)}, u32[]{:S(2)}) collective-permute-start(bf16[96,2048]{1,0:T(8,128)(2,1)S(1)} %get-tuple-element.146), channel_id=1, source_target_pairs={{0,8},{4,12},{8,0},{12,4},{1,9},{5,13},{9,1},{13,5},{2,10},{6,14},... | collective-permute-start | bytes 1179656 | tf_op jit(solution)/shard_map/ppermute | solution.py:29
  32.8 27.0 %collective-permute-start.14 = (bf16[96,2048]{1,0:T(8,128)(2,1)S(1)}, bf16[96,2048]{1,0:T(8,128)(2,1)S(1)}, u32[]{:S(2)}, u32[]{:S(2)}) collective-permute-start(bf16[96,2048]{1,0:T(8,128)(2,1)S(1)} %get-tuple-element.147), channel_id=1, source_target_pairs={{0,12},{4,8},{8,4},{12,0},{1,13},{5,9},{9,5},{13,1},{2,14},{6,10},... | collective-permute-start | bytes 1179656 | tf_op jit(solution)/shard_map/ppermute | solution.py:29
  34.1 61.9 %slice-start = ((s8[8388608]{0:T(1024)(128)(4,1)}), s8[4194304]{0:T(1024)(128)(4,1)S(1)}, s32[]{:S(2)}) async-start(s8[8388608]{0:T(1024)(128)(4,1)} %bitcast.18), calls=%async_computation | async-start | bytes 8388608
  34.1 34.8 %collective-permute-start.12 = (bf16[112,2048]{1,0:T(8,128)(2,1)S(1)}, bf16[112,2048]{1,0:T(8,128)(2,1)S(1)}, u32[]{:S(2)}, u32[]{:S(2)}) collective-permute-start(bf16[112,2048]{1,0:T(8,128)(2,1)S(1)} %get-tuple-element.144), channel_id=1, source_target_pairs={{0,4},{4,0},{8,12},{12,8},{1,5},{5,1},{9,13},{13,9},{2,6},{6,2},{1... | collective-permute-start | bytes 1376264 | tf_op jit(solution)/shard_map/ppermute | solution.py:29
  67.0 9.6 %collective-permute-start.22 = (bf16[96,128]{1,0:T(8,128)(2,1)S(1)}, bf16[96,128]{1,0:T(8,128)(2,1)S(1)}, u32[]{:S(2)}, u32[]{:S(2)}) collective-permute-start(bf16[96,128]{1,0:T(8,128)(2,1)S(1)} %get-tuple-element.159), channel_id=1, source_target_pairs={{0,1},{1,0},{2,3},{3,2},{4,5},{5,4},{6,7},{7,6},{8,9},{9,8},{10,11... | collective-permute-start | bytes 73736 | tf_op jit(solution)/shard_map/ppermute | solution.py:29
  67.1 10.0 %collective-permute-start.23 = (bf16[96,128]{1,0:T(8,128)(2,1)S(1)}, bf16[96,128]{1,0:T(8,128)(2,1)S(1)}, u32[]{:S(2)}, u32[]{:S(2)}) collective-permute-start(bf16[96,128]{1,0:T(8,128)(2,1)S(1)} %get-tuple-element.160), channel_id=1, source_target_pairs={{0,2},{1,3},{2,0},{3,1},{4,6},{5,7},{6,4},{7,5},{8,10},{9,11},{10,... | collective-permute-start | bytes 73736 | tf_op jit(solution)/shard_map/ppermute | solution.py:29
  68.9 9.9 %collective-permute-start.24 = (bf16[96,128]{1,0:T(8,128)(2,1)S(1)}, bf16[96,128]{1,0:T(8,128)(2,1)S(1)}, u32[]{:S(2)}, u32[]{:S(2)}) collective-permute-start(bf16[96,128]{1,0:T(8,128)(2,1)S(1)} %get-tuple-element.161), channel_id=1, source_target_pairs={{0,3},{1,2},{2,1},{3,0},{4,7},{5,6},{6,5},{7,4},{8,11},{9,10},{10,... | collective-permute-start | bytes 73736 | tf_op jit(solution)/shard_map/ppermute | solution.py:29
  69.0 27.0 %slice-start.1 = ((s8[8388608]{0:T(1024)(128)(4,1)}), s8[4194304]{0:T(1024)(128)(4,1)S(1)}, s32[]{:S(2)}) async-start(s8[8388608]{0:T(1024)(128)(4,1)} %bitcast.18), calls=%async_computation.1 | async-start | bytes 8388608
  76.6 27.2 %copy-start.1 = (s32[256,1]{0,1:T(1,128)S(1)}, s32[256,1]{0,1:T(1,128)}, u32[]{:S(2)}) copy-start(s32[256,1]{0,1:T(1,128)} %param.11) | copy-start | bytes 3076
  76.6 27.2 %copy-start.2 = (s32[64]{0:T(128)S(1)}, s32[64]{0:T(128)}, u32[]{:S(2)}) copy-start(s32[64]{0:T(128)} %param.12) | copy-start | bytes 772
  76.7 6.2 %collective-permute-start.18 = (bf16[112,128]{1,0:T(8,128)(2,1)S(1)}, bf16[112,128]{1,0:T(8,128)(2,1)S(1)}, u32[]{:S(2)}, u32[]{:S(2)}) collective-permute-start(bf16[112,128]{1,0:T(8,128)(2,1)S(1)} %get-tuple-element.152), channel_id=1, source_target_pairs={{0,1},{1,0},{2,3},{3,2},{4,5},{5,4},{6,7},{7,6},{8,9},{9,8},{10,11... | collective-permute-start | bytes 86024 | tf_op jit(solution)/shard_map/ppermute | solution.py:29
  77.1 16.5 %collective-permute-start.19 = (bf16[112,128]{1,0:T(8,128)(2,1)S(1)}, bf16[112,128]{1,0:T(8,128)(2,1)S(1)}, u32[]{:S(2)}, u32[]{:S(2)}) collective-permute-start(bf16[112,128]{1,0:T(8,128)(2,1)S(1)} %get-tuple-element.153), channel_id=1, source_target_pairs={{0,2},{1,3},{2,0},{3,1},{4,6},{5,7},{6,4},{7,5},{8,10},{9,11},{10,... | collective-permute-start | bytes 86024 | tf_op jit(solution)/shard_map/ppermute | solution.py:29
  78.8 15.3 %collective-permute-start.20 = (bf16[112,128]{1,0:T(8,128)(2,1)S(1)}, bf16[112,128]{1,0:T(8,128)(2,1)S(1)}, u32[]{:S(2)}, u32[]{:S(2)}) collective-permute-start(bf16[112,128]{1,0:T(8,128)(2,1)S(1)} %get-tuple-element.154), channel_id=1, source_target_pairs={{0,3},{1,2},{2,1},{3,0},{4,7},{5,6},{6,5},{7,4},{8,11},{9,10},{10,... | collective-permute-start | bytes 86024 | tf_op jit(solution)/shard_map/ppermute | solution.py:29
  82.9 18.7 %collective-permute-start.25 = (bf16[96,512]{1,0:T(8,128)(2,1)S(1)}, bf16[96,512]{1,0:T(8,128)(2,1)S(1)}, u32[]{:S(2)}, u32[]{:S(2)}) collective-permute-start(bf16[96,512]{1,0:T(8,128)(2,1)S(1)} %get-tuple-element.162), channel_id=1, source_target_pairs={{0,8},{4,12},{8,0},{12,4},{1,9},{5,13},{9,1},{13,5},{2,10},{6,14},... | collective-permute-start | bytes 294920 | tf_op jit(solution)/shard_map/ppermute | solution.py:29
  93.6 8.0 %collective-permute-start.26 = (bf16[96,512]{1,0:T(8,128)(2,1)S(1)}, bf16[96,512]{1,0:T(8,128)(2,1)S(1)}, u32[]{:S(2)}, u32[]{:S(2)}) collective-permute-start(bf16[96,512]{1,0:T(8,128)(2,1)S(1)} %get-tuple-element.163), channel_id=1, source_target_pairs={{0,12},{4,8},{8,4},{12,0},{1,13},{5,9},{9,5},{13,1},{2,14},{6,10},... | collective-permute-start | bytes 294920 | tf_op jit(solution)/shard_map/ppermute | solution.py:29
  95.8 8.1 %collective-permute-start.21 = (bf16[112,512]{1,0:T(8,128)(2,1)S(1)}, bf16[112,512]{1,0:T(8,128)(2,1)S(1)}, u32[]{:S(2)}, u32[]{:S(2)}) collective-permute-start(bf16[112,512]{1,0:T(8,128)(2,1)S(1)} %get-tuple-element.156), channel_id=1, source_target_pairs={{0,4},{4,0},{8,12},{12,8},{1,5},{5,1},{9,13},{13,9},{2,6},{6,2},{1... | collective-permute-start | bytes 344072 | tf_op jit(solution)/shard_map/ppermute | solution.py:29
  105.3 0.7 copy-start

commit v2 on v0

v2 whole, which is shorter than its diff:
```python
import functools

import jax
import jax.numpy as jnp
from jax import lax
from jax.experimental import pallas as pl
from jax.experimental.pallas import tpu as pltpu
from jax.sharding import PartitionSpec as P

KEY_VALUE_COLS = 1024
LANES = 128
MOST = 16
NEAR = 2
NEAR_ROWS = 112
FAR_ROWS = 96
LATER_ROWS = 32
VMEM = pltpu.VMEM
MIB = 1 << 20

f32, bf16, i32 = jnp.float32, jnp.bfloat16, jnp.int32


def first_counts(wide_size, local_count):
    most = -(-(local_count * MOST + 1) // 32) * 32
    return [min(NEAR_ROWS if k < NEAR else FAR_ROWS, most) for k in range(wide_size)]


def swap(x, axis, k):
    size = lax.axis_size(axis)
    return lax.ppermute(x, axis, [(i, i ^ k) for i in range(size)])


def after(x, *others):
    return lax.optimization_barrier((x, *others))[0]


def cost(flops, bytes_accessed):
    return pl.CostEstimate(flops=flops // 10, bytes_accessed=bytes_accessed // 10, transcendentals=0)


def params(mib):
    return pltpu.CompilerParams(vmem_limit_bytes=mib * MIB)


def rows_of(ref, start, count):
    return ref.at[pl.ds(start, count), :]


def pack_kernel(local_count, counts, before_counts, where_ref, tenant_ref, slot_ref, act_ref, *refs):
    wide_size = len(counts)
    place_ref, blocks = refs[0], refs[1 : 1 + wide_size]
    act_held, block_held, in_sem, out_sem = refs[1 + wide_size :]
    rows, features = act_held.shape
    chunks = in_sem.shape[0]
    width = features // chunks

    def load(c):
        cols = pl.ds(c * width, width)
        return pltpu.make_async_copy(act_ref.at[:, cols], act_held.at[:, cols], in_sem.at[c])

    for c in range(chunks):
        load(c).start()

    tenants = slot_ref.shape[1]
    tenant = tenant_ref[...]
    named = tenant == lax.broadcasted_iota(i32, (tenants, rows), 0)
    slots = jnp.broadcast_to(slot_ref[...].astype(f32), (8, tenants)).astype(bf16)
    slot = jnp.dot(slots, named.astype(f32).astype(bf16), preferred_element_type=f32)[:1]
    dest = jnp.floor((slot + 0.5) * (1.0 / local_count))
    adapter = slot - dest * local_count + 1.0
    leap = jnp.bitwise_xor(dest.astype(i32), where_ref[0])
    padded = max(8, wide_size)
    goes = (leap == lax.broadcasted_iota(i32, (padded, rows), 0)).astype(f32)
    earlier = lax.broadcasted_iota(i32, (rows, rows), 0) < lax.broadcasted_iota(
        i32, (rows, rows), 1
    )
    before = jnp.dot(
        goes.astype(bf16), earlier.astype(f32).astype(bf16), preferred_element_type=f32
    )
    position = jnp.sum(goes * before, axis=0, keepdims=True).astype(i32)
    adapters = jnp.broadcast_to(adapter, (8, rows)).astype(bf16)
    place = jnp.full((1, rows), -1, i32)
    more = jnp.zeros((1, rows), f32)
    offsets, here = [], []
    for k in range(wide_size):
        offsets.append(sum(counts[:k]))
        held = counts[k] - 1
        mine = position
        if before_counts is not None:
            mine = position - (before_counts[k] - 1) - (where_ref[2] - 1) * held
        more = jnp.where((leap == k) & (mine >= held), 1.0, more)
        mine = jnp.where((leap == k) & (mine >= 0) & (mine < held), mine, -1)
        place = jnp.where(mine >= 0, mine + offsets[k], place)
        here.append(mine)
    any_more = jnp.max(more, axis=1, keepdims=True)

    def store(k):
        return pltpu.make_async_copy(
            rows_of(block_held, offsets[k], counts[k]), blocks[k], out_sem.at[k]
        )

    for n, k in enumerate(reversed(range(wide_size))):
        count = counts[k]
        part = pl.ds(offsets[k], count)
        perm = (lax.broadcasted_iota(i32, (count, rows), 0) == here[k]).astype(f32).astype(bf16)
        filler = jnp.zeros((LANES - count, rows), bf16)
        ids = lax.dot_general(
            adapters,
            jnp.concatenate([perm, filler], axis=0),
            (((1,), (1,)), ((), ())),
            preferred_element_type=f32,
        )[:1]
        lane = lax.broadcasted_iota(i32, (1, LANES), 1)
        ids = jnp.where(lane == LANES - 1, any_more, ids)
        last = lax.broadcasted_iota(i32, (count, LANES), 0) == count - 1
        for c in range(chunks):
            cols = pl.ds(c * width, width)
            if n == 0:
                load(c).wait()
            body = jnp.dot(perm, act_held[:, cols], preferred_element_type=f32)
            if c == 0:
                first = jnp.where(last, ids, body[:, :LANES])
                body = jnp.concatenate([first, body[:, LANES:]], axis=1)
            block_held[part, cols] = body.astype(bf16)
        store(k).start()
    place_ref[...] = jnp.broadcast_to(place.astype(f32), (LANES, rows)).T
    for k in range(wide_size):
        store(k).wait()


def pack(where, tenant, slot, activations, local_count, counts, before_counts):
    rows, features = activations.shape
    wide_size = len(counts)
    chunks = 4
    anywhere = pl.BlockSpec(memory_space=pl.ANY)
    whole = pl.BlockSpec(memory_space=VMEM)
    return pl.pallas_call(
        functools.partial(pack_kernel, local_count, counts, before_counts),
        out_shape=[jax.ShapeDtypeStruct((rows, LANES), f32)]
        + [jax.ShapeDtypeStruct((c, features), bf16) for c in counts],
        in_specs=[pl.BlockSpec(memory_space=pltpu.SMEM), whole, whole, anywhere],
        out_specs=[whole] + [anywhere for _ in counts],
        scratch_shapes=[
            VMEM((rows, features), bf16),
            VMEM((sum(counts), features), bf16),
            pltpu.SemaphoreType.DMA((chunks,)),
            pltpu.SemaphoreType.DMA((wide_size,)),
        ],
        compiler_params=params(24),
        cost_estimate=cost(2 * sum(counts) * rows * features, 2 * features * (rows + sum(counts))),
        name="pack_rows",
    )(where, tenant, slot, activations)


def down_kernel(count, cols, narrow_size, per_step, where_ref, *refs):
    xs, weight_ref = refs[:count], refs[count]
    flag_ref, ids_ref = refs[count + 1 : count + 3]
    parts = refs[count + 3 : count + 3 + narrow_size]
    held_ref, weight_held, x_sem, weight_sem = refs[count + 3 + narrow_size :]
    steps = weight_sem.shape[0]

    offsets = [sum(x.shape[0] for x in xs[:n]) for n in range(count)]

    def load_x(n):
        return pltpu.make_async_copy(
            xs[n], rows_of(held_ref, offsets[n], xs[n].shape[0]), x_sem.at[n]
        )

    def load_weight(c):
        span = pl.ds(c * per_step, per_step)
        return pltpu.make_async_copy(weight_ref.at[span], weight_held.at[span], weight_sem.at[c])

    for n in range(count):
        load_x(n).start()
    for c in range(steps):
        load_weight(c).start()
    flag = jnp.zeros((1, LANES), f32)
    for n in range(count):
        load_x(n).wait()
        rows = xs[n].shape[0]
        last = held_ref[pl.ds(offsets[n] + rows - 16, 16), :LANES].astype(f32)[15:]
        flag = jnp.maximum(flag, last)
        turned = jnp.broadcast_to(last, (LANES, LANES)).T[:rows]
        keep = lax.broadcasted_iota(i32, (rows, LANES), 0) < rows - 1
        ids_ref[pl.ds(offsets[n], rows), :] = jnp.where(keep, turned, 0.0)
    lane = lax.broadcasted_iota(i32, (1, LANES), 1)
    flag_ref[0, 0] = jnp.max(jnp.where(lane == LANES - 1, flag, 0.0)).astype(i32)

    ids = ids_ref[...]
    total = jnp.zeros(ids.shape, f32)
    for c in range(steps):
        load_weight(c).wait()
        weights = jnp.concatenate(
            [weight_held[c * per_step + j] for j in range(per_step)], axis=1
        )
        found = jnp.dot(held_ref[...], weights, preferred_element_type=f32)
        for j in range(per_step):
            name = c * per_step + j + 1.0
            total = jnp.where(ids == name, found[:, j * LANES : (j + 1) * LANES], total)

    half = total.shape[0] // 2
    rank = LANES // 2
    top, bottom = total[:half], total[half:]
    low = lax.broadcasted_iota(i32, (half, LANES), 1) < rank
    keys = jnp.where(low, top, pltpu.roll(bottom, rank, 1))
    values = jnp.where(low, pltpu.roll(top, rank, 1), bottom)
    for j in range(narrow_size):
        start = jnp.bitwise_xor(where_ref[1], j) * cols
        parts[j][...] = jnp.where(start >= KEY_VALUE_COLS, values, keys).astype(parts[j].dtype)


def down(where, blocks, weight, cols, narrow_size):
    adapters, features, width = weight.shape
    rows = sum(b.shape[0] for b in blocks)
    per_step = min(4, adapters)
    anywhere = pl.BlockSpec(memory_space=pl.ANY)
    whole = pl.BlockSpec(memory_space=VMEM)
    scalar = pl.BlockSpec(memory_space=pltpu.SMEM)
    return pl.pallas_call(
        functools.partial(down_kernel, len(blocks), cols, narrow_size, per_step),
        out_shape=[
            jax.ShapeDtypeStruct((1, 1), i32),
            jax.ShapeDtypeStruct((rows, LANES), f32),
        ]
        + [jax.ShapeDtypeStruct((rows // 2, LANES), bf16 if j else f32) for j in range(narrow_size)],
        in_specs=[scalar] + [anywhere for _ in blocks] + [anywhere],
        out_specs=[scalar, whole] + [whole for _ in range(narrow_size)],
        scratch_shapes=[
            VMEM((rows, features), bf16),
            VMEM(weight.shape, bf16),
            pltpu.SemaphoreType.DMA((len(blocks),)),
            pltpu.SemaphoreType.DMA((adapters // per_step,)),
        ],
        compiler_params=params(32),
        cost_estimate=cost(2 * rows * features * adapters * width, 2 * features * (rows + adapters * width)),
        name="down_maps",
    )(where, *blocks, weight)


def up_kernel(narrow_size, ids_ref, *refs):
    parts, weight_ref, outs = refs[:narrow_size], refs[narrow_size], refs[narrow_size + 1 :]
    total = parts[0][...]
    for part in parts[1:]:
        total = total + part[...].astype(f32)
    low_rank = total.astype(bf16).astype(f32)
    rank = LANES // 2
    turned = pltpu.roll(low_rank, rank, 1)
    low = lax.broadcasted_iota(i32, low_rank.shape, 1) < rank
    twice = jnp.concatenate(
        [jnp.where(low, low_rank, turned), jnp.where(low, turned, low_rank)], axis=0
    )
    ids = ids_ref[...]
    second = (lax.broadcasted_iota(i32, ids.shape, 1) >= rank).astype(f32)
    adapters = weight_ref.shape[0] // rank
    left = [
        jnp.where(ids - second == 2.0 * pair + 1.0, twice, 0.0).astype(bf16)
        for pair in range(adapters // 2)
    ]
    found = jnp.dot(jnp.concatenate(left, axis=1), weight_ref[...], preferred_element_type=f32)
    offset = 0
    for out in outs:
        rows = out.shape[0]
        out[...] = found[offset : offset + rows].astype(bf16)
        offset += rows


def up(ids, parts, weight, counts):
    cols = weight.shape[1]
    return pl.pallas_call(
        functools.partial(up_kernel, len(parts)),
        out_shape=[jax.ShapeDtypeStruct((c, cols), bf16) for c in counts],
        compiler_params=params(24),
        cost_estimate=cost(2 * sum(counts) * weight.size, 2 * weight.size + 2 * sum(counts) * (cols + 512)),
        name="up_maps",
    )(ids, *parts, weight)


def base_kernel(count, where_ref, *refs):
    acts, weight_ref, out_ref = refs[:count], refs[count], refs[count + 1]
    step = pl.program_id(0)
    for j in range(count):

        @pl.when(step == j)
        def _(j=j):
            found = jnp.dot(acts[j][...], weight_ref[...], preferred_element_type=f32)
            out_ref[...] = found if j == 0 else out_ref[...] + found


def base(where, acts, weight):
    rows, features = acts[0].shape
    cols = weight.shape[1]
    count = len(acts)
    return pl.pallas_call(
        functools.partial(base_kernel, count),
        grid_spec=pltpu.PrefetchScalarGridSpec(
            num_scalar_prefetch=1,
            grid=(count,),
            in_specs=[pl.BlockSpec((rows, features), lambda i, where: (0, 0)) for _ in acts]
            + [
                pl.BlockSpec(
                    (features, cols), lambda i, where: (jnp.bitwise_xor(where[1], i), 0)
                )
            ],
            out_specs=pl.BlockSpec((rows, cols), lambda i, where: (0, 0)),
        ),
        out_shape=jax.ShapeDtypeStruct((rows, cols), f32),
        compiler_params=params(24),
        cost_estimate=cost(2 * rows * weight.size, 2 * weight.size + 2 * rows * features * count),
        name="shared_projection",
    )(where, *acts, weight)


def join_kernel(base_ref, place_ref, *refs):
    corrections, out_ref = refs[:-1], refs[-1]
    stacked = jnp.concatenate([c[...] for c in corrections], axis=0)
    rows, count = base_ref.shape[0], stacked.shape[0]
    place = place_ref[:, :1].astype(i32)
    perm = (lax.broadcasted_iota(i32, (rows, count), 1) == place).astype(f32).astype(bf16)
    found = jnp.dot(perm, stacked, preferred_element_type=f32)
    out_ref[...] = (base_ref[...] + found).astype(out_ref.dtype)


def join(base_out, place, corrections, dtype):
    rows, cols = base_out.shape
    count = sum(c.shape[0] for c in corrections)
    return pl.pallas_call(
        join_kernel,
        out_shape=jax.ShapeDtypeStruct((rows, cols), dtype),
        compiler_params=params(24),
        cost_estimate=cost(2 * rows * cols * count, 2 * cols * (count + 3 * rows)),
        name="join_corrections",
    )(base_out, place, *corrections)


def low_rank_parts(where, blocks, down_weight, cols, narrow_size):
    more, ids, *parts = down(where, blocks, down_weight, cols, narrow_size)
    return ids, more[0, 0], parts


def raise_parts(ids, parts, up_weight, counts):
    parts = [swap(p, "narrow", j) if j else p for j, p in enumerate(parts)]
    return up(ids, parts, up_weight, counts)


def later_turn(turn, axes, total, counts, tenant, slot, activations, down_weight, up_weight):
    wide_size, narrow_size = lax.axis_size("wide"), lax.axis_size("narrow")
    where = jnp.stack([*axes, turn])
    place, *sent = pack(
        where, tenant, slot, activations, down_weight.shape[0], [LATER_ROWS] * wide_size, counts
    )
    got = [swap(b, "wide", k) if k else b for k, b in enumerate(sent)]
    ids, more, parts = low_rank_parts(where, got, down_weight, up_weight.shape[1], narrow_size)
    outs = raise_parts(ids, parts, up_weight, [b.shape[0] for b in got])
    answers = [swap(b, "wide", k) if k else b for k, b in enumerate(outs)]
    return join(total, place, answers, f32), more


def on_device(
    activations,
    request_tenants,
    adapter_slot,
    shared_weight,
    adapter_down_weight,
    adapter_up_weight,
):
    rows = activations.shape[0]
    wide_size, narrow_size = lax.axis_size("wide"), lax.axis_size("narrow")
    local_count = adapter_down_weight.shape[0]
    axes = (lax.axis_index("wide").astype(i32), lax.axis_index("narrow").astype(i32))
    where = jnp.stack([*axes, jnp.int32(0)])
    tenant = request_tenants.reshape(1, rows)
    slot = adapter_slot.reshape(1, -1)
    up_weight = adapter_up_weight.reshape(-1, adapter_up_weight.shape[-1])

    cols = up_weight.shape[1]
    counts = first_counts(wide_size, local_count)
    place, *sent = pack(where, tenant, slot, activations, local_count, counts, None)
    got = [swap(b, "wide", k) if k else b for k, b in enumerate(sent)]

    bit = narrow_size // 2
    spread = {0: activations, bit: swap(after(activations, *sent), "narrow", bit)}
    ids, more, parts = low_rank_parts(where, got, adapter_down_weight, cols, narrow_size)
    bit //= 2
    while bit:
        spread.update({j ^ bit: swap(after(x, *parts), "narrow", bit) for j, x in list(spread.items())})
        bit //= 2
    answers = raise_parts(ids, parts, up_weight, counts)
    acts = [after(spread[j], *answers) for j in range(narrow_size)]
    base_out = base(where, acts, shared_weight)
    answers = [swap(answers[k], "wide", k) if k else answers[k] for k in range(wide_size)]

    def done(base_out):
        return join(base_out, place, answers, bf16)

    def go_on(base_out):
        def turn_of(state):
            turn, _, total = state
            total, more = later_turn(
                turn, axes, total, counts, tenant, slot, activations, adapter_down_weight, up_weight
            )
            return turn + 1, more, total

        state = (jnp.int32(1), jnp.int32(1), join(base_out, place, answers, f32))
        return lax.while_loop(lambda s: s[1] > 0, turn_of, state)[2].astype(bf16)

    return lax.cond(more > 0, go_on, done, base_out)


def solution(mesh):
    in_specs = (
        P(("groups", "wide"), "narrow"),
        P(("groups", "wide"), None),
        P(),
        P(None, "narrow"),
        P("wide", "narrow", None),
        P("wide", None, "narrow"),
    )
    out_specs = P(("groups", "wide"), "narrow")
    return jax.shard_map(
        on_device, mesh=mesh, in_specs=in_specs, out_specs=out_specs, check_vma=False
    )
```

time: 240 us -> 72.4 us (0.30)
  waiting for transfers between devices: 176 us -> 34.1 us
  matrix products: 18.9 us -> 0 us
  Pallas kernels: 0 us -> 17.6 us
  between operations: 13.5 us -> 0.77 us
  blocking collectives: 11.8 us -> 0 us
  starting transfers between devices: 9.79 us -> 19.7 us
  local copies, waits for them, and re-layouts: 7.6 us -> 0.02 us
    all_to_all x2 -> x0, waiting for transfers between devices: 174 us -> none  [the longest x1 159 us: on_device(): lax.all_to_all(outgoing, 'wide', split_axis=0, concat_axis=0, tiled=True)]
    ppermute x0 -> x12, waiting for transfers between devices: none -> 34.1 us  [swap(): return lax.ppermute(x, axis, [(i, i ^ k) for i in range(size)])]
    ppermute x0 -> x12, starting transfers between devices: none -> 19.7 us  [swap(): return lax.ppermute(x, axis, [(i, i ^ k) for i in range(size)])]
    dot_general x4 -> x0, matrix products: 18.9 us -> none  [the longest x1 7.69 us: on_device(): jnp.dot(lax.all_gather(activations, 'narrow', axis=1, tiled=True), shared...]
    pallas_call x0 -> x5, Pallas kernels: none -> 17.6 us  [the longest x1 7.39 us: down(): pl.pallas_call(functools.partial(down_kernel, len(blocks), cols, narrow_s...]
    psum x1 -> x0, blocking collectives: 11.8 us -> none  [on_device(): reduced_rank_output = lax.psum(own_rows, 'narrow').astype(jnp.bfloat16)]
    all_to_all x2 -> x0, starting transfers between devices: 9.79 us -> none  [the longest x1 6.32 us: on_device(): lax.all_to_all(outgoing, 'wide', split_axis=0, concat_axis=0, tiled=True)]
    scatter x1 -> x0, local copies, waits for them, and re-layouts: 5.51 us -> none  [on_device(): outgoing = jnp.zeros((tenant_count * MOST, feature_count), activations.dt...]
  transfers between devices with their start and end apart: 4 -> 12, of which waited for: 2 -> 5; matrix products, arithmetic and copies ran while one was open for 9% -> 0% of each run, Pallas kernels for 0% -> 16%
where the time goes in v2:
time: 72.4 us; the launch traced here: 72.2 us
  waiting for transfers between devices  34.1 us (47%)
  starting transfers between devices  19.7 us (27%)
  Pallas kernels  17.6 us (24%)
  between operations  0.77 us (1%)
    ppermute x12, waiting for transfers between devices, swap(): return lax.ppermute(x, axis, [(i, i ^ k) for i in range(size)])  34.1 us
    ppermute x12, starting transfers between devices, swap(): return lax.ppermute(x, axis, [(i, i ^ k) for i in range(size)])  19.7 us
    pallas_call x1, Pallas kernels, down(): pl.pallas_call(functools.partial(down_kernel, len(blocks), cols, narrow_s...  7.39 us
    pallas_call x1, Pallas kernels, pack(): pl.pallas_call(functools.partial(pack_kernel, local_count, counts, before...  5 us
    pallas_call x1, Pallas kernels, base(): pl.pallas_call(functools.partial(base_kernel, count), grid_spec=pltpu.Pre...  3.47 us
  transfers between devices with their start and end apart: 12, of which 5 were waited for; matrix products, arithmetic and copies ran while one was open for 0% of the time, Pallas kernels for 16%

profile of v2, /device:TPU:0, one launch (start us, length us, event | category | flops | bytes accessed | tf_op | source)
XLA Modules:
  0.0 72.2 jit_solution(16527019909605161575)
XLA Ops:
  0.0 0.1 pad_add_fusion.1.where_ref
  0.1 5.0 %pack_rows.2 = (f32[256,128]{1,0:T(8,128)S(1)}, bf16[112,2048]{1,0:T(8,128)(2,1)S(1)}, bf16[112,2048]{1,0:T(8,128)(2,1)S(1)}, bf16[96,2048]{1,0:T(8,128)(2,1)S(1)}, bf16[96,2048]{1,0:T(8,128)(2,1)S(1)}) custom-call(s32[3]{0:T(128)S(1)} %pad_add_fusion.1.where_ref, s32[1,256]{1,0:T(1,128)} %bitcast.20, s32[1,64]{1,0:T(1,128)} %bitcast.22, bf16[256,2048]{1,0:T(8,128)(2,1)} %refs_0_), custom_call_target="tpu_custom_call" | custom-call | flops 43620760 | bytes 275251 | tf_op jit(solution)/shard_map/pack_rows/pallas_call | solution.py:137
  5.1 3.0 %collective-permute-start.16 = (bf16[256,2048]{1,0:T(8,128)(2,1)}, bf16[256,2048]{1,0:T(8,128)(2,1)S(1)}, u32[]{:S(2)}, u32[]{:S(2)}) collective-permute-start(bf16[256,2048]{1,0:T(8,128)(2,1)} %refs_0_), channel_id=1, source_target_pairs={{0,2},{1,3},{2,0},{3,1},{4,6},{5,7},{6,4},{7,5},{8,10},{9,11},{10,... | collective-permute-start | bytes 3145736 | tf_op jit(solution)/shard_map/ppermute | solution.py:30
  8.1 1.6 %collective-permute-start.9 = (bf16[112,2048]{1,0:T(8,128)(2,1)S(1)}, bf16[112,2048]{1,0:T(8,128)(2,1)S(1)}, u32[]{:S(2)}, u32[]{:S(2)}) collective-permute-start(bf16[112,2048]{1,0:T(8,128)(2,1)S(1)} %get-tuple-element.154), channel_id=1, source_target_pairs={{0,4},{4,0},{8,12},{12,8},{1,5},{5,1},{9,13},{13,9},{2,6},{6,2},{1... | collective-permute-start | bytes 1376264 | tf_op jit(solution)/shard_map/ppermute | solution.py:30
  9.7 2.6 %collective-permute-start.10 = (bf16[96,2048]{1,0:T(8,128)(2,1)S(1)}, bf16[96,2048]{1,0:T(8,128)(2,1)S(1)}, u32[]{:S(2)}, u32[]{:S(2)}) collective-permute-start(bf16[96,2048]{1,0:T(8,128)(2,1)S(1)} %get-tuple-element.155), channel_id=1, source_target_pairs={{0,8},{4,12},{8,0},{12,4},{1,9},{5,13},{9,1},{13,5},{2,10},{6,14},... | collective-permute-start | bytes 1179656 | tf_op jit(solution)/shard_map/ppermute | solution.py:30
  12.3 0.2 collective-permute-start.11
  12.5 27.0 %collective-permute-done.10.refs_2_ = bf16[96,2048]{1,0:T(8,128)(2,1)S(1)} collective-permute-done((bf16[96,2048]{1,0:T(8,128)(2,1)S(1)}, bf16[96,2048]{1,0:T(8,128)(2,1)S(1)}, u32[]{:S(2)}, u32[]{:S(2)}) %collective-permute-start.10) | collective-permute-done | bytes 393248 | tf_op jit(solution)/shard_map/ppermute | solution.py:30
  39.5 7.4 %down_maps.2 = (s32[1,1]{1,0:T(1,128)}, f32[416,128]{1,0:T(8,128)S(1)}, f32[208,128]{1,0:T(8,128)S(1)}, bf16[208,128]{1,0:T(8,128)(2,1)S(1)}, bf16[208,128]{1,0:...) custom-call(s32[3]{0:T(128)S(1)} %pad_add_fusion.1.where_ref, bf16[112,2048]{1,0:T(8,128)(2,1)S(1)} %get-tuple-element.153.refs_0_, ...), custom_call_target="tpu_custom_call" | custom-call | flops 348966080 | bytes 1009254 | tf_op jit(solution)/shard_map/down_maps/pallas_call | solution.py:219
  46.9 0.1 collective-permute-start.15
  47.0 0.5 collective-permute-start.17
  47.5 0.1 collective-permute-start.12
  47.6 0.5 collective-permute-start.13
  48.1 1.3 %collective-permute-start.14 = (bf16[208,128]{1,0:T(8,128)(2,1)S(1)}, bf16[208,128]{1,0:T(8,128)(2,1)S(1)}, u32[]{:S(2)}, u32[]{:S(2)}) collective-permute-start(bf16[208,128]{1,0:T(8,128)(2,1)S(1)} %get-tuple-element.162), channel_id=1, source_target_pairs={{0,3},{1,2},{2,1},{3,0},{4,7},{5,6},{6,5},{7,4},{8,11},{9,10},{10,... | collective-permute-start | bytes 159752 | tf_op jit(solution)/shard_map/ppermute | solution.py:30
  49.4 1.8 %collective-permute-done.12.refs_1_ = bf16[208,128]{1,0:T(8,128)(2,1)S(1)} collective-permute-done((bf16[208,128]{1,0:T(8,128)(2,1)S(1)}, bf16[208,128]{1,0:T(8,128)(2,1)S(1)}, u32[]{:S(2)}, u32[]{:S(2)}) %collective-permute-start.12) | collective-permute-done | bytes 53280 | tf_op jit(solution)/shard_map/ppermute | solution.py:30
  51.2 1.0 %collective-permute-done.13.refs_2_ = bf16[208,128]{1,0:T(8,128)(2,1)S(1)} collective-permute-done((bf16[208,128]{1,0:T(8,128)(2,1)S(1)}, bf16[208,128]{1,0:T(8,128)(2,1)S(1)}, u32[]{:S(2)}, u32[]{:S(2)}) %collective-permute-start.13) | collective-permute-done | bytes 53280 | tf_op jit(solution)/shard_map/ppermute | solution.py:30
  52.2 0.2 collective-permute-done.14.refs_3_
  52.4 0.7 up_maps.2
  53.1 7.3 %collective-permute-start.18 = (bf16[112,512]{1,0:T(8,128)(2,1)S(1)}, bf16[112,512]{1,0:T(8,128)(2,1)S(1)}, u32[]{:S(2)}, u32[]{:S(2)}) collective-permute-start(bf16[112,512]{1,0:T(8,128)(2,1)S(1)} %get-tuple-element.164), channel_id=1, source_target_pairs={{0,4},{4,0},{8,12},{12,8},{1,5},{5,1},{9,13},{13,9},{2,6},{6,2},{1... | collective-permute-start | bytes 344072 | tf_op jit(solution)/shard_map/ppermute | solution.py:30
  60.4 1.1 %collective-permute-start.19 = (bf16[96,512]{1,0:T(8,128)(2,1)S(1)}, bf16[96,512]{1,0:T(8,128)(2,1)S(1)}, u32[]{:S(2)}, u32[]{:S(2)}) collective-permute-start(bf16[96,512]{1,0:T(8,128)(2,1)S(1)} %get-tuple-element.165), channel_id=1, source_target_pairs={{0,8},{4,12},{8,0},{12,4},{1,9},{5,13},{9,1},{13,5},{2,10},{6,14},... | collective-permute-start | bytes 294920 | tf_op jit(solution)/shard_map/ppermute | solution.py:30
  61.5 1.4 %collective-permute-start.20 = (bf16[96,512]{1,0:T(8,128)(2,1)S(1)}, bf16[96,512]{1,0:T(8,128)(2,1)S(1)}, u32[]{:S(2)}, u32[]{:S(2)}) collective-permute-start(bf16[96,512]{1,0:T(8,128)(2,1)S(1)} %get-tuple-element.166), channel_id=1, source_target_pairs={{0,12},{4,8},{8,4},{12,0},{1,13},{5,9},{9,5},{13,1},{2,14},{6,10},... | collective-permute-start | bytes 294920 | tf_op jit(solution)/shard_map/ppermute | solution.py:30
  63.6 3.5 %shared_projection.1 = f32[256,512]{1,0:T(8,128)S(1)} custom-call(s32[3]{0:T(128)S(1)} %pad_add_fusion.1.where_ref, bf16[256,2048]{1,0:T(8,128)(2,1)S(1)} %copy-done.1, bf16[256,2048]{1,0:T(8,128)(2,1)S(1)} %collective-permute-done.15.refs_1_, bf16[256,2048]{1,0:T(8,128)(2,1)S(1)} %collective-permute-done.16.refs_2_, ...), custom_call_target="tpu_custom_call" | custom-call | flops 214748368 | bytes 1258291 | tf_op jit(solution)/shard_map/shared_projection/pallas_call | solution.py:293
  67.1 4.1 %collective-permute-done.19 = bf16[96,512]{1,0:T(8,128)(2,1)S(1)} collective-permute-done((bf16[96,512]{1,0:T(8,128)(2,1)S(1)}, bf16[96,512]{1,0:T(8,128)(2,1)S(1)}, u32[]{:S(2)}, u32[]{:S(2)}) %collective-permute-start.19) | collective-permute-done | bytes 98336 | tf_op jit(solution)/shard_map/ppermute | solution.py:30
  71.2 1.1 %conditional.1 = (bf16[256,512]{1,0:T(8,128)(2,1)}) conditional(s32[]{:T(128)} %bitcast.8, (f32[256,512]{1,0:T(8,128)S(1)}, f32[256,128]{1,0:T(8,128)S(1)}, bf16[112,512]{1,0:T(8,128)(2,1)S(1)}, bf16[112,512]{1,0:T(8,128)(2,1)S(1)}, bf16[96,512]{1,0:T(8,128)(2,1)S(1)}, /*index=5*/bf16[96,512]{1,0:T(8,128)(2,1)S(1)}) %tuple.29, ...), branch_computations={%region_0.0_spmd, %region_1.0_spmd} | conditional | flops 148609424 | bytes 6177427 | solution.py:406
  71.2 1.1 %join_corrections.3 = bf16[256,512]{1,0:T(8,128)(2,1)} custom-call(f32[256,512]{1,0:T(8,128)S(1)} %get-tuple-element.86.base_ref, f32[256,128]{1,0:T(8,128)S(1)} %get-tuple-element.87.place_ref, bf16[112,512]{1,0:T(8,128)(2,1)S(1)} %get-tuple-element.88.refs_0_, bf16[112,512]{1,0:T(8,128)(2,1)S(1)} %get-tuple-element.89.refs_1_, ...), custom_call_target="tpu_custom_call" | custom-call | flops 10905190 | bytes 121241 | tf_op jit(solution)/shard_map/cond/branch_0_fun/join_corrections/pallas_call | solution.py:326
  (17 shorter events, 0.0 us)
Async XLA Ops:
  0.0 46.9 %copy-start.1 = (bf16[256,2048]{1,0:T(8,128)(2,1)S(1)}, bf16[256,2048]{1,0:T(8,128)(2,1)}, u32[]{:S(2)}) copy-start(bf16[256,2048]{1,0:T(8,128)(2,1)} %refs_0_) | copy-start | bytes 3145732
  0.0 52.4 %copy-start.2 = (bf16[16,64,512]{2,1,0:T(8,128)(2,1)S(1)}, bf16[16,64,512]{2,1,0:T(8,128)(2,1)}, u32[]{:S(2)}) copy-start(bf16[16,64,512]{2,1,0:T(8,128)(2,1)} %param.15) | copy-start | bytes 3145732
  0.0 63.6 %copy-start = (bf16[8192,512]{1,0:T(8,128)(2,1)S(1)}, bf16[8192,512]{1,0:T(8,128)(2,1)}, u32[]{:S(2)}) copy-start(bf16[8192,512]{1,0:T(8,128)(2,1)} %refs_4_.3) | copy-start | bytes 25165828
  5.1 41.9 %collective-permute-start.16 = (bf16[256,2048]{1,0:T(8,128)(2,1)}, bf16[256,2048]{1,0:T(8,128)(2,1)S(1)}, u32[]{:S(2)}, u32[]{:S(2)}) collective-permute-start(bf16[256,2048]{1,0:T(8,128)(2,1)} %refs_0_), channel_id=1, source_target_pairs={{0,2},{1,3},{2,0},{3,1},{4,6},{5,7},{6,4},{7,5},{8,10},{9,11},{10,... | collective-permute-start | bytes 3145736 | tf_op jit(solution)/shard_map/ppermute | solution.py:30
  8.1 31.4 %collective-permute-start.9 = (bf16[112,2048]{1,0:T(8,128)(2,1)S(1)}, bf16[112,2048]{1,0:T(8,128)(2,1)S(1)}, u32[]{:S(2)}, u32[]{:S(2)}) collective-permute-start(bf16[112,2048]{1,0:T(8,128)(2,1)S(1)} %get-tuple-element.154), channel_id=1, source_target_pairs={{0,4},{4,0},{8,12},{12,8},{1,5},{5,1},{9,13},{13,9},{2,6},{6,2},{1... | collective-permute-start | bytes 1376264 | tf_op jit(solution)/shard_map/ppermute | solution.py:30
  9.7 29.8 %collective-permute-start.10 = (bf16[96,2048]{1,0:T(8,128)(2,1)S(1)}, bf16[96,2048]{1,0:T(8,128)(2,1)S(1)}, u32[]{:S(2)}, u32[]{:S(2)}) collective-permute-start(bf16[96,2048]{1,0:T(8,128)(2,1)S(1)} %get-tuple-element.155), channel_id=1, source_target_pairs={{0,8},{4,12},{8,0},{12,4},{1,9},{5,13},{9,1},{13,5},{2,10},{6,14},... | collective-permute-start | bytes 1179656 | tf_op jit(solution)/shard_map/ppermute | solution.py:30
  12.3 27.2 %collective-permute-start.11 = (bf16[96,2048]{1,0:T(8,128)(2,1)S(1)}, bf16[96,2048]{1,0:T(8,128)(2,1)S(1)}, u32[]{:S(2)}, u32[]{:S(2)}) collective-permute-start(bf16[96,2048]{1,0:T(8,128)(2,1)S(1)} %get-tuple-element.156), channel_id=1, source_target_pairs={{0,12},{4,8},{8,4},{12,0},{1,13},{5,9},{9,5},{13,1},{2,14},{6,10},... | collective-permute-start | bytes 1179656 | tf_op jit(solution)/shard_map/ppermute | solution.py:30
  46.9 24.3 %copy-start.5 = (s32[256,1]{0,1:T(1,128)S(1)}, s32[256,1]{0,1:T(1,128)}, u32[]{:S(2)}) copy-start(s32[256,1]{0,1:T(1,128)} %param.11) | copy-start | bytes 3076
  46.9 24.3 %copy-start.6 = (s32[64]{0:T(128)S(1)}, s32[64]{0:T(128)}, u32[]{:S(2)}) copy-start(s32[64]{0:T(128)} %param.12) | copy-start | bytes 772
  46.9 16.7 %collective-permute-start.15 = (bf16[256,2048]{1,0:T(8,128)(2,1)S(1)}, bf16[256,2048]{1,0:T(8,128)(2,1)S(1)}, u32[]{:S(2)}, u32[]{:S(2)}) collective-permute-start(bf16[256,2048]{1,0:T(8,128)(2,1)S(1)} %copy-done.1), channel_id=1, source_target_pairs={{0,1},{1,0},{2,3},{3,2},{4,5},{5,4},{6,7},{7,6},{8,9},{9,8},{10,11... | collective-permute-start | bytes 3145736 | tf_op jit(solution)/shard_map/ppermute | solution.py:30
  47.0 16.6 %collective-permute-start.17 = (bf16[256,2048]{1,0:T(8,128)(2,1)S(1)}, bf16[256,2048]{1,0:T(8,128)(2,1)S(1)}, u32[]{:S(2)}, u32[]{:S(2)}) collective-permute-start(bf16[256,2048]{1,0:T(8,128)(2,1)S(1)} %collective-permute-done.16.refs_2_), channel_id=1, source_target_pairs={{0,1},{1,0},{2,3},{3,2},{4,5},{5,4},{6,7},{7,6},{8,9},{9,8},{10,11... | collective-permute-start | bytes 3145736 | tf_op jit(solution)/shard_map/ppermute | solution.py:30
  47.5 3.7 %collective-permute-start.12 = (bf16[208,128]{1,0:T(8,128)(2,1)S(1)}, bf16[208,128]{1,0:T(8,128)(2,1)S(1)}, u32[]{:S(2)}, u32[]{:S(2)}) collective-permute-start(bf16[208,128]{1,0:T(8,128)(2,1)S(1)} %get-tuple-element.160), channel_id=1, source_target_pairs={{0,1},{1,0},{2,3},{3,2},{4,5},{5,4},{6,7},{7,6},{8,9},{9,8},{10,11... | collective-permute-start | bytes 159752 | tf_op jit(solution)/shard_map/ppermute | solution.py:30
  47.6 4.6 %collective-permute-start.13 = (bf16[208,128]{1,0:T(8,128)(2,1)S(1)}, bf16[208,128]{1,0:T(8,128)(2,1)S(1)}, u32[]{:S(2)}, u32[]{:S(2)}) collective-permute-start(bf16[208,128]{1,0:T(8,128)(2,1)S(1)} %get-tuple-element.161), channel_id=1, source_target_pairs={{0,2},{1,3},{2,0},{3,1},{4,6},{5,7},{6,4},{7,5},{8,10},{9,11},{10,... | collective-permute-start | bytes 159752 | tf_op jit(solution)/shard_map/ppermute | solution.py:30
  48.1 4.3 %collective-permute-start.14 = (bf16[208,128]{1,0:T(8,128)(2,1)S(1)}, bf16[208,128]{1,0:T(8,128)(2,1)S(1)}, u32[]{:S(2)}, u32[]{:S(2)}) collective-permute-start(bf16[208,128]{1,0:T(8,128)(2,1)S(1)} %get-tuple-element.162), channel_id=1, source_target_pairs={{0,3},{1,2},{2,1},{3,0},{4,7},{5,6},{6,5},{7,4},{8,11},{9,10},{10,... | collective-permute-start | bytes 159752 | tf_op jit(solution)/shard_map/ppermute | solution.py:30
  53.1 18.0 %collective-permute-start.18 = (bf16[112,512]{1,0:T(8,128)(2,1)S(1)}, bf16[112,512]{1,0:T(8,128)(2,1)S(1)}, u32[]{:S(2)}, u32[]{:S(2)}) collective-permute-start(bf16[112,512]{1,0:T(8,128)(2,1)S(1)} %get-tuple-element.164), channel_id=1, source_target_pairs={{0,4},{4,0},{8,12},{12,8},{1,5},{5,1},{9,13},{13,9},{2,6},{6,2},{1... | collective-permute-start | bytes 344072 | tf_op jit(solution)/shard_map/ppermute | solution.py:30
  60.4 10.7 %collective-permute-start.19 = (bf16[96,512]{1,0:T(8,128)(2,1)S(1)}, bf16[96,512]{1,0:T(8,128)(2,1)S(1)}, u32[]{:S(2)}, u32[]{:S(2)}) collective-permute-start(bf16[96,512]{1,0:T(8,128)(2,1)S(1)} %get-tuple-element.165), channel_id=1, source_target_pairs={{0,8},{4,12},{8,0},{12,4},{1,9},{5,13},{9,1},{13,5},{2,10},{6,14},... | collective-permute-start | bytes 294920 | tf_op jit(solution)/shard_map/ppermute | solution.py:30
  61.5 9.6 %collective-permute-start.20 = (bf16[96,512]{1,0:T(8,128)(2,1)S(1)}, bf16[96,512]{1,0:T(8,128)(2,1)S(1)}, u32[]{:S(2)}, u32[]{:S(2)}) collective-permute-start(bf16[96,512]{1,0:T(8,128)(2,1)S(1)} %get-tuple-element.166), channel_id=1, source_target_pairs={{0,12},{4,8},{8,4},{12,0},{1,13},{5,9},{9,5},{13,1},{2,14},{6,10},... | collective-permute-start | bytes 294920 | tf_op jit(solution)/shard_map/ppermute | solution.py:30

commit v3 on v2

--- a/solution.py
+++ b/solution.py
@@ -48,8 +48,8 @@
 
 def pack_kernel(local_count, counts, before_counts, where_ref, tenant_ref, slot_ref, act_ref, *refs):
     wide_size = len(counts)
-    place_ref, blocks = refs[0], refs[1 : 1 + wide_size]
-    act_held, block_held, in_sem, out_sem = refs[1 + wide_size :]
+    begun_ref, place_ref, blocks = refs[0], refs[1], refs[2 : 2 + wide_size]
+    act_held, in_sem = refs[2 + wide_size :]
     rows, features = act_held.shape
     chunks = in_sem.shape[0]
     width = features // chunks
@@ -60,6 +60,7 @@
 
     for c in range(chunks):
         load(c).start()
+    begun_ref[0, 0] = jnp.int32(1)
 
     tenants = slot_ref.shape[1]
     tenant = tenant_ref[...]
@@ -94,14 +95,8 @@
         here.append(mine)
     any_more = jnp.max(more, axis=1, keepdims=True)
 
-    def store(k):
-        return pltpu.make_async_copy(
-            rows_of(block_held, offsets[k], counts[k]), blocks[k], out_sem.at[k]
-        )
-
     for n, k in enumerate(reversed(range(wide_size))):
         count = counts[k]
-        part = pl.ds(offsets[k], count)
         perm = (lax.broadcasted_iota(i32, (count, rows), 0) == here[k]).astype(f32).astype(bf16)
         filler = jnp.zeros((LANES - count, rows), bf16)
         ids = lax.dot_general(
@@ -121,12 +116,8 @@
             if c == 0:
                 first = jnp.where(last, ids, body[:, :LANES])
                 body = jnp.concatenate([first, body[:, LANES:]], axis=1)
-            block_held[part, cols] = body.astype(bf16)
-        store(k).start()
+            blocks[k][:, cols] = body.astype(bf16)
     place_ref[...] = jnp.broadcast_to(place.astype(f32), (LANES, rows)).T
-    for k in range(wide_size):
-        store(k).wait()
-
 
 def pack(where, tenant, slot, activations, local_count, counts, before_counts):
     rows, features = activations.shape
@@ -134,50 +125,64 @@
     chunks = 4
     anywhere = pl.BlockSpec(memory_space=pl.ANY)
     whole = pl.BlockSpec(memory_space=VMEM)
+    scalar = pl.BlockSpec(memory_space=pltpu.SMEM)
     return pl.pallas_call(
         functools.partial(pack_kernel, local_count, counts, before_counts),
-        out_shape=[jax.ShapeDtypeStruct((rows, LANES), f32)]
+        out_shape=[
+            jax.ShapeDtypeStruct((1, 1), i32),
+            jax.ShapeDtypeStruct((rows, LANES), f32),
+        ]
         + [jax.ShapeDtypeStruct((c, features), bf16) for c in counts],
-        in_specs=[pl.BlockSpec(memory_space=pltpu.SMEM), whole, whole, anywhere],
-        out_specs=[whole] + [anywhere for _ in counts],
-        scratch_shapes=[
-            VMEM((rows, features), bf16),
-            VMEM((sum(counts), features), bf16),
-            pltpu.SemaphoreType.DMA((chunks,)),
-            pltpu.SemaphoreType.DMA((wide_size,)),
-        ],
+        in_specs=[scalar, whole, whole, anywhere],
+        out_specs=[scalar, whole] + [whole for _ in counts],
+        scratch_shapes=[VMEM((rows, features), bf16), pltpu.SemaphoreType.DMA((chunks,))],
         compiler_params=params(24),
         cost_estimate=cost(2 * sum(counts) * rows * features, 2 * features * (rows + sum(counts))),
         name="pack_rows",
     )(where, tenant, slot, activations)
 
 
+def stage_kernel(weight_ref, out_ref, sem):
+    adapters, _, width = weight_ref.shape
+
+    def load(j):
+        return pltpu.make_async_copy(
+            weight_ref.at[j], out_ref.at[:, pl.ds(j * width, width)], sem.at[j]
+        )
+
+    for j in range(adapters):
+        load(j).start()
+    for j in range(adapters):
+        load(j).wait()
+
+
+def stage(weight):
+    adapters, features, width = weight.shape
+    return pl.pallas_call(
+        stage_kernel,
+        out_shape=pltpu.VMEM((features, adapters * width), weight.dtype),
+        in_specs=[pl.BlockSpec(memory_space=pl.ANY)],
+        out_specs=pl.BlockSpec(memory_space=VMEM),
+        scratch_shapes=[pltpu.SemaphoreType.DMA((adapters,))],
+        compiler_params=params(16),
+        cost_estimate=cost(1, 4 * weight.size),
+        name="stage_down_maps",
+    )(weight)
+
+
 def down_kernel(count, cols, narrow_size, per_step, where_ref, *refs):
     xs, weight_ref = refs[:count], refs[count]
     flag_ref, ids_ref = refs[count + 1 : count + 3]
     parts = refs[count + 3 : count + 3 + narrow_size]
-    held_ref, weight_held, x_sem, weight_sem = refs[count + 3 + narrow_size :]
-    steps = weight_sem.shape[0]
+    (held_ref,) = refs[count + 3 + narrow_size :]
+    steps = weight_ref.shape[1] // (per_step * LANES)
 
     offsets = [sum(x.shape[0] for x in xs[:n]) for n in range(count)]
 
-    def load_x(n):
-        return pltpu.make_async_copy(
-            xs[n], rows_of(held_ref, offsets[n], xs[n].shape[0]), x_sem.at[n]
-        )
-
-    def load_weight(c):
-        span = pl.ds(c * per_step, per_step)
-        return pltpu.make_async_copy(weight_ref.at[span], weight_held.at[span], weight_sem.at[c])
-
-    for n in range(count):
-        load_x(n).start()
-    for c in range(steps):
-        load_weight(c).start()
     flag = jnp.zeros((1, LANES), f32)
     for n in range(count):
-        load_x(n).wait()
         rows = xs[n].shape[0]
+        held_ref[pl.ds(offsets[n], rows), :] = xs[n][...]
         last = held_ref[pl.ds(offsets[n] + rows - 16, 16), :LANES].astype(f32)[15:]
         flag = jnp.maximum(flag, last)
         turned = jnp.broadcast_to(last, (LANES, LANES)).T[:rows]
@@ -189,10 +194,7 @@
     ids = ids_ref[...]
     total = jnp.zeros(ids.shape, f32)
     for c in range(steps):
-        load_weight(c).wait()
-        weights = jnp.concatenate(
-            [weight_held[c * per_step + j] for j in range(per_step)], axis=1
-        )
+        weights = weight_ref[:, c * per_step * LANES : (c + 1) * per_step * LANES]
         found = jnp.dot(held_ref[...], weights, preferred_element_type=f32)
         for j in range(per_step):
             name = c * per_step + j + 1.0
@@ -210,10 +212,9 @@
 
 
 def down(where, blocks, weight, cols, narrow_size):
-    adapters, features, width = weight.shape
+    features, width = weight.shape
     rows = sum(b.shape[0] for b in blocks)
-    per_step = min(4, adapters)
-    anywhere = pl.BlockSpec(memory_space=pl.ANY)
+    per_step = min(4, width // LANES)
     whole = pl.BlockSpec(memory_space=VMEM)
     scalar = pl.BlockSpec(memory_space=pltpu.SMEM)
     return pl.pallas_call(
@@ -223,16 +224,11 @@
             jax.ShapeDtypeStruct((rows, LANES), f32),
         ]
         + [jax.ShapeDtypeStruct((rows // 2, LANES), bf16 if j else f32) for j in range(narrow_size)],
-        in_specs=[scalar] + [anywhere for _ in blocks] + [anywhere],
+        in_specs=[scalar] + [whole for _ in blocks] + [whole],
         out_specs=[scalar, whole] + [whole for _ in range(narrow_size)],
-        scratch_shapes=[
-            VMEM((rows, features), bf16),
-            VMEM(weight.shape, bf16),
-            pltpu.SemaphoreType.DMA((len(blocks),)),
-            pltpu.SemaphoreType.DMA((adapters // per_step,)),
-        ],
+        scratch_shapes=[VMEM((rows, features), bf16)],
         compiler_params=params(32),
-        cost_estimate=cost(2 * rows * features * adapters * width, 2 * features * (rows + adapters * width)),
+        cost_estimate=cost(2 * rows * features * width, 2 * features * (rows + width)),
         name="down_maps",
     )(where, *blocks, weight)
 
@@ -345,11 +341,12 @@
 def later_turn(turn, axes, total, counts, tenant, slot, activations, down_weight, up_weight):
     wide_size, narrow_size = lax.axis_size("wide"), lax.axis_size("narrow")
     where = jnp.stack([*axes, turn])
-    place, *sent = pack(
+    _, place, *sent = pack(
         where, tenant, slot, activations, down_weight.shape[0], [LATER_ROWS] * wide_size, counts
     )
     got = [swap(b, "wide", k) if k else b for k, b in enumerate(sent)]
-    ids, more, parts = low_rank_parts(where, got, down_weight, up_weight.shape[1], narrow_size)
+    staged = stage(down_weight)
+    ids, more, parts = low_rank_parts(where, got, staged, up_weight.shape[1], narrow_size)
     outs = raise_parts(ids, parts, up_weight, [b.shape[0] for b in got])
     answers = [swap(b, "wide", k) if k else b for k, b in enumerate(outs)]
     return join(total, place, answers, f32), more
@@ -374,19 +371,28 @@
 
     cols = up_weight.shape[1]
     counts = first_counts(wide_size, local_count)
-    place, *sent = pack(where, tenant, slot, activations, local_count, counts, None)
+    begun, place, *sent = pack(where, tenant, slot, activations, local_count, counts, None)
     got = [swap(b, "wide", k) if k else b for k, b in enumerate(sent)]
 
-    bit = narrow_size // 2
-    spread = {0: activations, bit: swap(after(activations, *sent), "narrow", bit)}
-    ids, more, parts = low_rank_parts(where, got, adapter_down_weight, cols, narrow_size)
-    bit //= 2
-    while bit:
-        spread.update({j ^ bit: swap(after(x, *parts), "narrow", bit) for j, x in list(spread.items())})
-        bit //= 2
+    def beside_rows(activations, shared_weight, down_weight):
+        spread = {0: activations}
+        bit = narrow_size // 2
+        while bit:
+            spread.update({j ^ bit: swap(x, "narrow", bit) for j, x in list(spread.items())})
+            bit //= 2
+        return base(where, [spread[j] for j in range(narrow_size)], shared_weight), stage(down_weight)
+
+    def never(activations, shared_weight, down_weight):
+        adapters, features, width = down_weight.shape
+        return jnp.zeros((rows, cols), f32), jnp.zeros((features, adapters * width), bf16)
+
+    base_out, staged = lax.cond(
+        begun[0, 0] > 0, beside_rows, never, activations, shared_weight, adapter_down_weight
+    )
+    ids, more, parts = low_rank_parts(
+        where, [after(b, base_out) for b in got], staged, cols, narrow_size
+    )
     answers = raise_parts(ids, parts, up_weight, counts)
-    acts = [after(spread[j], *answers) for j in range(narrow_size)]
-    base_out = base(where, acts, shared_weight)
     answers = [swap(answers[k], "wide", k) if k else answers[k] for k in range(wide_size)]
 
     def done(base_out):

time: 72.4 us -> 72 us (level)
  starting transfers between devices: 19.7 us -> 13.8 us
  local copies, waits for them, and re-layouts: 0.02 us -> 3.21 us
  Pallas kernels: 17.6 us -> 19 us
    ppermute x12, starting transfers between devices: 19.7 us -> 13.8 us  [swap(): return lax.ppermute(x, axis, [(i, i ^ k) for i in range(size)])]
    pallas_call x0 -> x1, Pallas kernels: none -> 3.66 us  [stage(): pl.pallas_call(stage_kernel, out_shape=pltpu.VMEM((features, adapters * w...]
    pallas_call x1, Pallas kernels: 7.39 us -> 4.78 us  [down(): pl.pallas_call(functools.partial(down_kernel, len(blocks), cols, narrow_s...]
    cond x0 -> x4, local copies, waits for them, and re-layouts: none -> 2.5 us
    pallas_call x1, Pallas kernels: 5 us -> 2.93 us  [pack(): pl.pallas_call(functools.partial(pack_kernel, local_count, counts, before...]
    pallas_call x1, Pallas kernels: 0.65 us -> 1.88 us  [up(): pl.pallas_call(functools.partial(up_kernel, len(parts)), out_shape=[jax.S...]
    pallas_call x1, Pallas kernels: 3.47 us -> 4.35 us  [base(): pl.pallas_call(functools.partial(base_kernel, count), grid_spec=pltpu.Pre...]
  transfers between devices with their start and end apart: 12 -> 12, of which waited for: 5 -> 4; matrix products, arithmetic and copies ran while one was open for 0% -> 0% of each run, Pallas kernels for 16% -> 11%
where the time goes in v3:
time: 72 us; the launch traced here: 71.8 us
  waiting for transfers between devices  34.3 us (48%)
  Pallas kernels  19 us (26%)
  starting transfers between devices  13.8 us (19%)
  local copies, waits for them, and re-layouts  3.21 us (4%)
  between operations  1.35 us (2%)
    ppermute x12, waiting for transfers between devices, swap(): return lax.ppermute(x, axis, [(i, i ^ k) for i in range(size)])  34.3 us
    ppermute x12, starting transfers between devices, swap(): return lax.ppermute(x, axis, [(i, i ^ k) for i in range(size)])  13.8 us
    pallas_call x1, Pallas kernels, down(): pl.pallas_call(functools.partial(down_kernel, len(blocks), cols, narrow_s...  4.78 us
    pallas_call x1, Pallas kernels, base(): pl.pallas_call(functools.partial(base_kernel, count), grid_spec=pltpu.Pre...  4.35 us
    pallas_call x1, Pallas kernels, stage(): pl.pallas_call(stage_kernel, out_shape=pltpu.VMEM((features, adapters * w...  3.66 us
    pallas_call x1, Pallas kernels, pack(): pl.pallas_call(functools.partial(pack_kernel, local_count, counts, before...  2.93 us
    cond x4, local copies, waits for them, and re-layouts  2.5 us
    pallas_call x1, Pallas kernels, up(): pl.pallas_call(functools.partial(up_kernel, len(parts)), out_shape=[jax.S...  1.88 us
  transfers between devices with their start and end apart: 12, of which 4 were waited for; matrix products, arithmetic and copies ran while one was open for 0% of the time, Pallas kernels for 11%

profile of v3, /device:TPU:0, one launch (start us, length us, event | category | flops | bytes accessed | tf_op | source)
XLA Modules:
  0.0 71.8 jit_solution(111859741785663533)
XLA Ops:
  0.0 0.1 pad_add_fusion.1.where_ref
  0.1 2.9 %pack_rows.4 = (s32[1,1]{1,0:T(1,128)}, f32[256,128]{1,0:T(8,128)S(1)}, bf16[112,2048]{1,0:T(8,128)(2,1)S(1)}, bf16[112,2048]{1,0:T(8,128)(2,1)S(1)}, bf16[96,20...) custom-call(s32[3]{0:T(128)S(1)} %pad_add_fusion.1.where_ref, s32[1,256]{1,0:T(1,128)} %bitcast.19, s32[1,64]{1,0:T(1,128)} %bitcast.21, ...), custom_call_target="tpu_custom_call" | custom-call | flops 43620760 | bytes 275251 | tf_op jit(solution)/shard_map/pack_rows/pallas_call | solution.py:129
  3.0 3.1 %collective-permute-start.12 = (bf16[112,2048]{1,0:T(8,128)(2,1)S(1)}, bf16[112,2048]{1,0:T(8,128)(2,1)S(1)}, u32[]{:S(2)}, u32[]{:S(2)}) collective-permute-start(bf16[112,2048]{1,0:T(8,128)(2,1)S(1)} %get-tuple-element.224), channel_id=1, source_target_pairs={{0,4},{4,0},{8,12},{12,8},{1,5},{5,1},{9,13},{13,9},{2,6},{6,2},{1... | collective-permute-start | bytes 1376264 | tf_op jit(solution)/shard_map/ppermute | solution.py:30
  6.1 2.5 %collective-permute-start.14 = (bf16[96,2048]{1,0:T(8,128)(2,1)S(1)}, bf16[96,2048]{1,0:T(8,128)(2,1)S(1)}, u32[]{:S(2)}, u32[]{:S(2)}) collective-permute-start(bf16[96,2048]{1,0:T(8,128)(2,1)S(1)} %get-tuple-element.228), channel_id=1, source_target_pairs={{0,12},{4,8},{8,4},{12,0},{1,13},{5,9},{9,5},{13,1},{2,14},{6,10},... | collective-permute-start | bytes 1179656 | tf_op jit(solution)/shard_map/ppermute | solution.py:30
  8.6 0.1 collective-permute-start.13
  9.3 35.2 %conditional.2 = (f32[256,512]{1,0:T(8,128)}, bf16[2048,2048]{1,0:T(8,128)(2,1)S(1)}) conditional(s32[]{:T(128)} %bitcast.8, () %tuple.34, (bf16[256,2048]{1,0:T(8,128)(2,1)}, s32[3]{0:T(128)S(1)}, bf16[8192,512]{1,0:T(8,128)(2,1)}, bf16[16,2048,128]{2,1,0:T(8,128)(2,1)}) %tuple.35), branch_computations={%region_0.0_spmd, %region_1.0_spmd} | conditional | flops 214748368 | bytes 53267852 | solution.py:389
  9.3 1.6 %collective-permute-start.1 = (bf16[256,2048]{1,0:T(8,128)(2,1)}, bf16[256,2048]{1,0:T(8,128)(2,1)S(1)}, u32[]{:S(2)}, u32[]{:S(2)}) collective-permute-start(bf16[256,2048]{1,0:T(8,128)(2,1)} %get-tuple-element.150.refs_0_), channel_id=1, source_target_pairs={{0,2},{1,3},{2,0},{3,1},{4,6},{5,7},{6,4},{7,5},{8,10},{9,11},{10,... | collective-permute-start | bytes 3145736 | tf_op jit(solution)/shard_map/cond/branch_1_fun/ppermute | solution.py:30
  10.9 23.1 %collective-permute-done.1.refs_2_ = bf16[256,2048]{1,0:T(8,128)(2,1)S(1)} collective-permute-done((bf16[256,2048]{1,0:T(8,128)(2,1)}, bf16[256,2048]{1,0:T(8,128)(2,1)S(1)}, u32[]{:S(2)}, u32[]{:S(2)}) %collective-permute-start.1) | collective-permute-done | bytes 1048608 | tf_op jit(solution)/shard_map/cond/branch_1_fun/ppermute | solution.py:30
  34.0 3.7 %stage_down_maps.2 = bf16[2048,2048]{1,0:T(8,128)(2,1)S(1)} custom-call(bf16[16,2048,128]{2,1,0:T(8,128)(2,1)} %get-tuple-element.152.weight_ref), custom_call_target="tpu_custom_call" | custom-call | bytes 1677721 | tf_op jit(solution)/shard_map/cond/branch_1_fun/stage_down_maps/pallas_call | solution.py:161
  37.7 2.5 %copy-done.3 = bf16[8192,512]{1,0:T(8,128)(2,1)S(1)} copy-done((bf16[8192,512]{1,0:T(8,128)(2,1)S(1)}, bf16[8192,512]{1,0:T(8,128)(2,1)}, u32[]{:S(2)}) %copy-start.3) | copy-done | bytes 8388632 | tf_op jit(solution)/shard_map/cond
  40.2 4.3 %shared_projection.1 = f32[256,512]{1,0:T(8,128)} custom-call(s32[3]{0:T(128)S(1)} %get-tuple-element.149.where_ref, bf16[256,2048]{1,0:T(8,128)(2,1)S(1)} %copy-done.2, bf16[256,2048]{1,0:T(8,128)(2,1)S(1)} %collective-permute-done.refs_1_, bf16[256,2048]{1,0:T(8,128)(2,1)S(1)} %collective-permute-done.1.refs_2_, ...), custom_call_target="tpu_custom_call" | custom-call | flops 214748368 | bytes 1258291 | tf_op jit(solution)/shard_map/cond/branch_1_fun/shared_projection/pallas_call | solution.py:289
  44.5 4.8 %down_maps.4 = (s32[1,1]{1,0:T(1,128)}, f32[416,128]{1,0:T(8,128)S(1)}, f32[208,128]{1,0:T(8,128)S(1)}, bf16[208,128]{1,0:T(8,128)(2,1)S(1)}, bf16[208,128]{1,0:...) custom-call(s32[3]{0:T(128)S(1)} %pad_add_fusion.1.where_ref, bf16[112,2048]{1,0:T(8,128)(2,1)S(1)} %get-tuple-element.223.refs_0_, ...), custom_call_target="tpu_custom_call" | custom-call | flops 348966080 | bytes 1009254 | tf_op jit(solution)/shard_map/down_maps/pallas_call | solution.py:220
  49.3 0.6 collective-permute-start.15
  49.9 1.5 %collective-permute-start.16 = (bf16[208,128]{1,0:T(8,128)(2,1)S(1)}, bf16[208,128]{1,0:T(8,128)(2,1)S(1)}, u32[]{:S(2)}, u32[]{:S(2)}) collective-permute-start(bf16[208,128]{1,0:T(8,128)(2,1)S(1)} %get-tuple-element.236), channel_id=1, source_target_pairs={{0,2},{1,3},{2,0},{3,1},{4,6},{5,7},{6,4},{7,5},{8,10},{9,11},{10,... | collective-permute-start | bytes 159752 | tf_op jit(solution)/shard_map/ppermute | solution.py:30
  51.4 2.6 %collective-permute-done.16.refs_2_ = bf16[208,128]{1,0:T(8,128)(2,1)S(1)} collective-permute-done((bf16[208,128]{1,0:T(8,128)(2,1)S(1)}, bf16[208,128]{1,0:T(8,128)(2,1)S(1)}, u32[]{:S(2)}, u32[]{:S(2)}) %collective-permute-start.16) | collective-permute-done | bytes 53280 | tf_op jit(solution)/shard_map/ppermute | solution.py:30
  54.0 1.5 %collective-permute-done.17.refs_3_ = bf16[208,128]{1,0:T(8,128)(2,1)S(1)} collective-permute-done((bf16[208,128]{1,0:T(8,128)(2,1)S(1)}, bf16[208,128]{1,0:T(8,128)(2,1)S(1)}, u32[]{:S(2)}, u32[]{:S(2)}) %collective-permute-start.17) | collective-permute-done | bytes 53280 | tf_op jit(solution)/shard_map/ppermute | solution.py:30
  55.5 1.9 %up_maps.4 = (bf16[112,512]{1,0:T(8,128)(2,1)S(1)}, bf16[112,512]{1,0:T(8,128)(2,1)S(1)}, bf16[96,512]{1,0:T(8,128)(2,1)S(1)}, bf16[96,512]{1,0:T(8,128)(2,1)S(1)}) custom-call(f32[416,128]{1,0:T(8,128)S(1)} %get-tuple-element.233.ids_ref, f32[208,128]{1,0:T(8,128)S(1)} %get-tuple-element.234.refs_0_, bf16[208,128]{1,0:T(8,128)(2,1)S(1)} %collective-permute-done.15.refs_1_, ...), custom_call_target="tpu_custom_call" | custom-call | flops 43620760 | bytes 190054 | tf_op jit(solution)/shard_map/up_maps/pallas_call | solution.py:265
  57.4 1.6 %collective-permute-start.18 = (bf16[112,512]{1,0:T(8,128)(2,1)S(1)}, bf16[112,512]{1,0:T(8,128)(2,1)S(1)}, u32[]{:S(2)}, u32[]{:S(2)}) collective-permute-start(bf16[112,512]{1,0:T(8,128)(2,1)S(1)} %get-tuple-element.239), channel_id=1, source_target_pairs={{0,4},{4,0},{8,12},{12,8},{1,5},{5,1},{9,13},{13,9},{2,6},{6,2},{1... | collective-permute-start | bytes 344072 | tf_op jit(solution)/shard_map/ppermute | solution.py:30
  59.0 1.7 %collective-permute-start.19 = (bf16[96,512]{1,0:T(8,128)(2,1)S(1)}, bf16[96,512]{1,0:T(8,128)(2,1)S(1)}, u32[]{:S(2)}, u32[]{:S(2)}) collective-permute-start(bf16[96,512]{1,0:T(8,128)(2,1)S(1)} %get-tuple-element.240), channel_id=1, source_target_pairs={{0,8},{4,12},{8,0},{12,4},{1,9},{5,13},{9,1},{13,5},{2,10},{6,14},... | collective-permute-start | bytes 294920 | tf_op jit(solution)/shard_map/ppermute | solution.py:30
  60.7 1.2 %collective-permute-start.20 = (bf16[96,512]{1,0:T(8,128)(2,1)S(1)}, bf16[96,512]{1,0:T(8,128)(2,1)S(1)}, u32[]{:S(2)}, u32[]{:S(2)}) collective-permute-start(bf16[96,512]{1,0:T(8,128)(2,1)S(1)} %get-tuple-element.241), channel_id=1, source_target_pairs={{0,12},{4,8},{8,4},{12,0},{1,13},{5,9},{9,5},{13,1},{2,14},{6,10},... | collective-permute-start | bytes 294920 | tf_op jit(solution)/shard_map/ppermute | solution.py:30
  62.5 7.1 %collective-permute-done.19 = bf16[96,512]{1,0:T(8,128)(2,1)S(1)} collective-permute-done((bf16[96,512]{1,0:T(8,128)(2,1)S(1)}, bf16[96,512]{1,0:T(8,128)(2,1)S(1)}, u32[]{:S(2)}, u32[]{:S(2)}) %collective-permute-start.19) | collective-permute-done | bytes 98336 | tf_op jit(solution)/shard_map/ppermute | solution.py:30
  69.7 1.4 %conditional.3 = (bf16[256,512]{1,0:T(8,128)(2,1)S(1)}) conditional(s32[]{:T(128)} %bitcast.9, (f32[256,512]{1,0:T(8,128)}, f32[256,128]{1,0:T(8,128)S(1)}, bf16[112,512]{1,0:T(8,128)(2,1)S(1)}, bf16[112,512]{1,0:T(8,128)(2,1)S(1)}, bf16[96,512]{1,0:T(8,128)(2,1)S(1)}, /*index=5*/bf16[96,512]{1,0:T(8,128)(2,1)S(1)}) %tuple.40, (f32[256,512]{1,0:T(8,128)}, ...), branch_computations={%region_2.0_spmd, %region_3.0_spmd} | conditional | flops 148609424 | bytes 40623120 | solution.py:412
  69.7 1.4 %join_corrections.5 = bf16[256,512]{1,0:T(8,128)(2,1)S(1)} custom-call(f32[256,512]{1,0:T(8,128)} %get-tuple-element.153.base_ref, f32[256,128]{1,0:T(8,128)S(1)} %get-tuple-element.154.place_ref, bf16[112,512]{1,0:T(8,128)(2,1)S(1)} %get-tuple-element.155.refs_0_, bf16[112,512]{1,0:T(8,128)(2,1)S(1)} %get-tuple-element.156.refs_1_, ...), custom_call_target="tpu_custom_call" | custom-call | flops 10905190 | bytes 121241 | tf_op jit(solution)/shard_map/cond/branch_0_fun/join_corrections/pallas_call | solution.py:322
  71.1 0.7 copy-done.4
  (21 shorter events, 0.1 us)
Async XLA Ops:
  3.0 41.5 %collective-permute-start.12 = (bf16[112,2048]{1,0:T(8,128)(2,1)S(1)}, bf16[112,2048]{1,0:T(8,128)(2,1)S(1)}, u32[]{:S(2)}, u32[]{:S(2)}) collective-permute-start(bf16[112,2048]{1,0:T(8,128)(2,1)S(1)} %get-tuple-element.224), channel_id=1, source_target_pairs={{0,4},{4,0},{8,12},{12,8},{1,5},{5,1},{9,13},{13,9},{2,6},{6,2},{1... | collective-permute-start | bytes 1376264 | tf_op jit(solution)/shard_map/ppermute | solution.py:30
  6.1 38.4 %collective-permute-start.14 = (bf16[96,2048]{1,0:T(8,128)(2,1)S(1)}, bf16[96,2048]{1,0:T(8,128)(2,1)S(1)}, u32[]{:S(2)}, u32[]{:S(2)}) collective-permute-start(bf16[96,2048]{1,0:T(8,128)(2,1)S(1)} %get-tuple-element.228), channel_id=1, source_target_pairs={{0,12},{4,8},{8,4},{12,0},{1,13},{5,9},{9,5},{13,1},{2,14},{6,10},... | collective-permute-start | bytes 1179656 | tf_op jit(solution)/shard_map/ppermute | solution.py:30
  8.6 35.9 %collective-permute-start.13 = (bf16[96,2048]{1,0:T(8,128)(2,1)S(1)}, bf16[96,2048]{1,0:T(8,128)(2,1)S(1)}, u32[]{:S(2)}, u32[]{:S(2)}) collective-permute-start(bf16[96,2048]{1,0:T(8,128)(2,1)S(1)} %get-tuple-element.226), channel_id=1, source_target_pairs={{0,8},{4,12},{8,0},{12,4},{1,9},{5,13},{9,1},{13,5},{2,10},{6,14},... | collective-permute-start | bytes 1179656 | tf_op jit(solution)/shard_map/ppermute | solution.py:30
  9.3 24.6 %collective-permute-start.1 = (bf16[256,2048]{1,0:T(8,128)(2,1)}, bf16[256,2048]{1,0:T(8,128)(2,1)S(1)}, u32[]{:S(2)}, u32[]{:S(2)}) collective-permute-start(bf16[256,2048]{1,0:T(8,128)(2,1)} %get-tuple-element.150.refs_0_), channel_id=1, source_target_pairs={{0,2},{1,3},{2,0},{3,1},{4,6},{5,7},{6,4},{7,5},{8,10},{9,11},{10,... | collective-permute-start | bytes 3145736 | tf_op jit(solution)/shard_map/cond/branch_1_fun/ppermute | solution.py:30
  10.9 26.7 %collective-permute-start = (bf16[256,2048]{1,0:T(8,128)(2,1)}, bf16[256,2048]{1,0:T(8,128)(2,1)S(1)}, u32[]{:S(2)}, u32[]{:S(2)}) collective-permute-start(bf16[256,2048]{1,0:T(8,128)(2,1)} %get-tuple-element.150.refs_0_), channel_id=1, source_target_pairs={{0,1},{1,0},{2,3},{3,2},{4,5},{5,4},{6,7},{7,6},{8,9},{9,8},{10,11... | collective-permute-start | bytes 3145736 | tf_op jit(solution)/shard_map/cond/branch_1_fun/ppermute | solution.py:30
  34.0 3.7 %collective-permute-start.2 = (bf16[256,2048]{1,0:T(8,128)(2,1)S(1)}, bf16[256,2048]{1,0:T(8,128)(2,1)S(1)}, u32[]{:S(2)}, u32[]{:S(2)}) collective-permute-start(bf16[256,2048]{1,0:T(8,128)(2,1)S(1)} %collective-permute-done.1.refs_2_), channel_id=1, source_target_pairs={{0,1},{1,0},{2,3},{3,2},{4,5},{5,4},{6,7},{7,6},{8,9},{9,8},{10,11... | collective-permute-start | bytes 3145736 | tf_op jit(solution)/shard_map/cond/branch_1_fun/ppermute | solution.py:30
  34.0 3.7 %copy-start.2 = (bf16[256,2048]{1,0:T(8,128)(2,1)S(1)}, bf16[256,2048]{1,0:T(8,128)(2,1)}, u32[]{:S(2)}) copy-start(bf16[256,2048]{1,0:T(8,128)(2,1)} %get-tuple-element.150.refs_0_) | copy-start | bytes 3145732 | tf_op jit(solution)/shard_map/cond
  34.0 6.2 %copy-start.3 = (bf16[8192,512]{1,0:T(8,128)(2,1)S(1)}, bf16[8192,512]{1,0:T(8,128)(2,1)}, u32[]{:S(2)}) copy-start(bf16[8192,512]{1,0:T(8,128)(2,1)} %get-tuple-element.243.refs_4_) | copy-start | bytes 25165828 | tf_op jit(solution)/shard_map/cond
  44.5 25.1 %copy-start.5 = (s32[256,1]{0,1:T(1,128)S(1)}, s32[256,1]{0,1:T(1,128)}, u32[]{:S(2)}) copy-start(s32[256,1]{0,1:T(1,128)} %param.13) | copy-start | bytes 3076
  44.5 25.1 %copy-start.6 = (s32[64]{0:T(128)S(1)}, s32[64]{0:T(128)}, u32[]{:S(2)}) copy-start(s32[64]{0:T(128)} %param.14) | copy-start | bytes 772
  44.5 25.1 %copy-start.1 = (bf16[256,2048]{1,0:T(8,128)(2,1)S(1)}, bf16[256,2048]{1,0:T(8,128)(2,1)}, u32[]{:S(2)}) copy-start(bf16[256,2048]{1,0:T(8,128)(2,1)} %act_ref.1) | copy-start | bytes 3145732
  49.3 2.1 %collective-permute-start.15 = (bf16[208,128]{1,0:T(8,128)(2,1)S(1)}, bf16[208,128]{1,0:T(8,128)(2,1)S(1)}, u32[]{:S(2)}, u32[]{:S(2)}) collective-permute-start(bf16[208,128]{1,0:T(8,128)(2,1)S(1)} %get-tuple-element.235), channel_id=1, source_target_pairs={{0,1},{1,0},{2,3},{3,2},{4,5},{5,4},{6,7},{7,6},{8,9},{9,8},{10,11... | collective-permute-start | bytes 159752 | tf_op jit(solution)/shard_map/ppermute | solution.py:30
  49.9 4.1 %collective-permute-start.16 = (bf16[208,128]{1,0:T(8,128)(2,1)S(1)}, bf16[208,128]{1,0:T(8,128)(2,1)S(1)}, u32[]{:S(2)}, u32[]{:S(2)}) collective-permute-start(bf16[208,128]{1,0:T(8,128)(2,1)S(1)} %get-tuple-element.236), channel_id=1, source_target_pairs={{0,2},{1,3},{2,0},{3,1},{4,6},{5,7},{6,4},{7,5},{8,10},{9,11},{10,... | collective-permute-start | bytes 159752 | tf_op jit(solution)/shard_map/ppermute | solution.py:30
  51.4 4.1 %collective-permute-start.17 = (bf16[208,128]{1,0:T(8,128)(2,1)S(1)}, bf16[208,128]{1,0:T(8,128)(2,1)S(1)}, u32[]{:S(2)}, u32[]{:S(2)}) collective-permute-start(bf16[208,128]{1,0:T(8,128)(2,1)S(1)} %get-tuple-element.237), channel_id=1, source_target_pairs={{0,3},{1,2},{2,1},{3,0},{4,7},{5,6},{6,5},{7,4},{8,11},{9,10},{10,... | collective-permute-start | bytes 159752 | tf_op jit(solution)/shard_map/ppermute | solution.py:30
  57.4 12.2 %collective-permute-start.18 = (bf16[112,512]{1,0:T(8,128)(2,1)S(1)}, bf16[112,512]{1,0:T(8,128)(2,1)S(1)}, u32[]{:S(2)}, u32[]{:S(2)}) collective-permute-start(bf16[112,512]{1,0:T(8,128)(2,1)S(1)} %get-tuple-element.239), channel_id=1, source_target_pairs={{0,4},{4,0},{8,12},{12,8},{1,5},{5,1},{9,13},{13,9},{2,6},{6,2},{1... | collective-permute-start | bytes 344072 | tf_op jit(solution)/shard_map/ppermute | solution.py:30
  59.0 10.7 %collective-permute-start.19 = (bf16[96,512]{1,0:T(8,128)(2,1)S(1)}, bf16[96,512]{1,0:T(8,128)(2,1)S(1)}, u32[]{:S(2)}, u32[]{:S(2)}) collective-permute-start(bf16[96,512]{1,0:T(8,128)(2,1)S(1)} %get-tuple-element.240), channel_id=1, source_target_pairs={{0,8},{4,12},{8,0},{12,4},{1,9},{5,13},{9,1},{13,5},{2,10},{6,14},... | collective-permute-start | bytes 294920 | tf_op jit(solution)/shard_map/ppermute | solution.py:30
  60.7 9.0 %collective-permute-start.20 = (bf16[96,512]{1,0:T(8,128)(2,1)S(1)}, bf16[96,512]{1,0:T(8,128)(2,1)S(1)}, u32[]{:S(2)}, u32[]{:S(2)}) collective-permute-start(bf16[96,512]{1,0:T(8,128)(2,1)S(1)} %get-tuple-element.241), channel_id=1, source_target_pairs={{0,12},{4,8},{8,4},{12,0},{1,13},{5,9},{9,5},{13,1},{2,14},{6,10},... | collective-permute-start | bytes 294920 | tf_op jit(solution)/shard_map/ppermute | solution.py:30
  71.1 0.7 copy-start.4

commit v4 on v3

--- a/solution.py
+++ b/solution.py
@@ -32,6 +32,10 @@
 
 def after(x, *others):
     return lax.optimization_barrier((x, *others))[0]
+
+
+def after_all(xs, *others):
+    return lax.optimization_barrier((tuple(xs), others))[0]
 
 
 def cost(flops, bytes_accessed):
@@ -136,38 +140,43 @@
         in_specs=[scalar, whole, whole, anywhere],
         out_specs=[scalar, whole] + [whole for _ in counts],
         scratch_shapes=[VMEM((rows, features), bf16), pltpu.SemaphoreType.DMA((chunks,))],
-        compiler_params=params(24),
+        compiler_params=params(12),
         cost_estimate=cost(2 * sum(counts) * rows * features, 2 * features * (rows + sum(counts))),
         name="pack_rows",
     )(where, tenant, slot, activations)
 
 
-def stage_kernel(weight_ref, out_ref, sem):
-    adapters, _, width = weight_ref.shape
-
-    def load(j):
-        return pltpu.make_async_copy(
-            weight_ref.at[j], out_ref.at[:, pl.ds(j * width, width)], sem.at[j]
+def stage_kernel(down_ref, up_ref, down_out, up_out, sem):
+    adapters, _, width = down_ref.shape
+    copies = [
+        pltpu.make_async_copy(
+            down_ref.at[j], down_out.at[:, pl.ds(j * width, width)], sem.at[j]
         )
-
-    for j in range(adapters):
-        load(j).start()
-    for j in range(adapters):
-        load(j).wait()
-
-
-def stage(weight):
-    adapters, features, width = weight.shape
+        for j in range(adapters)
+    ]
+    copies.append(pltpu.make_async_copy(up_ref, up_out, sem.at[adapters]))
+    for copy in copies:
+        copy.start()
+    for copy in copies:
+        copy.wait()
+
+
+def stage(down_weight, up_weight):
+    adapters, features, width = down_weight.shape
+    whole = pl.BlockSpec(memory_space=VMEM)
     return pl.pallas_call(
         stage_kernel,
-        out_shape=pltpu.VMEM((features, adapters * width), weight.dtype),
-        in_specs=[pl.BlockSpec(memory_space=pl.ANY)],
-        out_specs=pl.BlockSpec(memory_space=VMEM),
-        scratch_shapes=[pltpu.SemaphoreType.DMA((adapters,))],
-        compiler_params=params(16),
-        cost_estimate=cost(1, 4 * weight.size),
-        name="stage_down_maps",
-    )(weight)
+        out_shape=[
+            pltpu.VMEM((features, adapters * width), down_weight.dtype),
+            pltpu.VMEM(up_weight.shape, up_weight.dtype),
+        ],
+        in_specs=[pl.BlockSpec(memory_space=pl.ANY)] * 2,
+        out_specs=[whole, whole],
+        scratch_shapes=[pltpu.SemaphoreType.DMA((adapters + 1,))],
+        compiler_params=params(12),
+        cost_estimate=cost(10, 10),
+        name="stage_maps",
+    )(down_weight, up_weight)
 
 
 def down_kernel(count, cols, narrow_size, per_step, where_ref, *refs):
@@ -227,7 +236,7 @@
         in_specs=[scalar] + [whole for _ in blocks] + [whole],
         out_specs=[scalar, whole] + [whole for _ in range(narrow_size)],
         scratch_shapes=[VMEM((rows, features), bf16)],
-        compiler_params=params(32),
+        compiler_params=params(18),
         cost_estimate=cost(2 * rows * features * width, 2 * features * (rows + width)),
         name="down_maps",
     )(where, *blocks, weight)
@@ -265,27 +274,32 @@
     return pl.pallas_call(
         functools.partial(up_kernel, len(parts)),
         out_shape=[jax.ShapeDtypeStruct((c, cols), bf16) for c in counts],
-        compiler_params=params(24),
+        compiler_params=params(10),
         cost_estimate=cost(2 * sum(counts) * weight.size, 2 * weight.size + 2 * sum(counts) * (cols + 512)),
         name="up_maps",
     )(ids, *parts, weight)
 
 
 def base_kernel(count, where_ref, *refs):
-    acts, weight_ref, out_ref = refs[:count], refs[count], refs[count + 1]
+    acts, weight_ref, so_far, out_ref = refs[:count], refs[count], refs[count + 1 : -1], refs[-1]
     step = pl.program_id(0)
     for j in range(count):
 
         @pl.when(step == j)
         def _(j=j):
             found = jnp.dot(acts[j][...], weight_ref[...], preferred_element_type=f32)
-            out_ref[...] = found if j == 0 else out_ref[...] + found
-
-
-def base(where, acts, weight):
+            if j:
+                found = out_ref[...] + found
+            elif so_far:
+                found = so_far[0][...] + found
+            out_ref[...] = found
+
+
+def base(where, acts, first, stride, weight, so_far):
     rows, features = acts[0].shape
     cols = weight.shape[1]
     count = len(acts)
+    given = [] if so_far is None else [so_far]
     return pl.pallas_call(
         functools.partial(base_kernel, count),
         grid_spec=pltpu.PrefetchScalarGridSpec(
@@ -294,16 +308,18 @@
             in_specs=[pl.BlockSpec((rows, features), lambda i, where: (0, 0)) for _ in acts]
             + [
                 pl.BlockSpec(
-                    (features, cols), lambda i, where: (jnp.bitwise_xor(where[1], i), 0)
+                    (features, cols),
+                    lambda i, where: (jnp.bitwise_xor(where[1], first + i * stride), 0),
                 )
-            ],
+            ]
+            + [pl.BlockSpec((rows, cols), lambda i, where: (0, 0)) for _ in given],
             out_specs=pl.BlockSpec((rows, cols), lambda i, where: (0, 0)),
         ),
         out_shape=jax.ShapeDtypeStruct((rows, cols), f32),
-        compiler_params=params(24),
-        cost_estimate=cost(2 * rows * weight.size, 2 * weight.size + 2 * rows * features * count),
+        compiler_params=params(14),
+        cost_estimate=cost(2 * rows * features * count * cols, 2 * features * count * (cols + rows)),
         name="shared_projection",
-    )(where, *acts, weight)
+    )(where, *acts, weight, *given)
 
 
 def join_kernel(base_ref, place_ref, *refs):
@@ -322,20 +338,17 @@
     return pl.pallas_call(
         join_kernel,
         out_shape=jax.ShapeDtypeStruct((rows, cols), dtype),
-        compiler_params=params(24),
+        compiler_params=params(10),
         cost_estimate=cost(2 * rows * cols * count, 2 * cols * (count + 3 * rows)),
         name="join_corrections",
     )(base_out, place, *corrections)
 
 
-def low_rank_parts(where, blocks, down_weight, cols, narrow_size):
-    more, ids, *parts = down(where, blocks, down_weight, cols, narrow_size)
-    return ids, more[0, 0], parts
-
-
-def raise_parts(ids, parts, up_weight, counts):
+def answers_for(where, blocks, staged, narrow_size):
+    down_weight, up_weight = staged
+    more, ids, *parts = down(where, blocks, down_weight, up_weight.shape[1], narrow_size)
     parts = [swap(p, "narrow", j) if j else p for j, p in enumerate(parts)]
-    return up(ids, parts, up_weight, counts)
+    return up(ids, parts, up_weight, [b.shape[0] for b in blocks]), more
 
 
 def later_turn(turn, axes, total, counts, tenant, slot, activations, down_weight, up_weight):
@@ -345,11 +358,9 @@
         where, tenant, slot, activations, down_weight.shape[0], [LATER_ROWS] * wide_size, counts
     )
     got = [swap(b, "wide", k) if k else b for k, b in enumerate(sent)]
-    staged = stage(down_weight)
-    ids, more, parts = low_rank_parts(where, got, staged, up_weight.shape[1], narrow_size)
-    outs = raise_parts(ids, parts, up_weight, [b.shape[0] for b in got])
+    outs, more = answers_for(where, got, stage(down_weight, up_weight), narrow_size)
     answers = [swap(b, "wide", k) if k else b for k, b in enumerate(outs)]
-    return join(total, place, answers, f32), more
+    return join(total, place, answers, f32), more[0, 0]
 
 
 def on_device(
@@ -372,28 +383,56 @@
     cols = up_weight.shape[1]
     counts = first_counts(wide_size, local_count)
     begun, place, *sent = pack(where, tenant, slot, activations, local_count, counts, None)
-    got = [swap(b, "wide", k) if k else b for k, b in enumerate(sent)]
-
-    def beside_rows(activations, shared_weight, down_weight):
-        spread = {0: activations}
-        bit = narrow_size // 2
+    order = sorted(range(wide_size), key=lambda k: (k == wide_size // 2, -k))
+    early, late = (order[:-1], order[-1:]) if wide_size > 2 else (order, [])
+    got = {k: swap(sent[k], "wide", k) if k else sent[k] for k in order}
+    half = narrow_size // 2
+    across = swap(after(activations, *sent), "narrow", half) if half else None
+    maps = after_all((adapter_down_weight, up_weight), *sent)
+    staged = stage(*maps)
+
+    def step(work, *operands):
+        def never(*operands):
+            return jax.tree.map(
+                lambda s: jnp.zeros(s.shape, s.dtype), jax.eval_shape(work, *operands)
+            )
+
+        return lax.cond(begun[0, 0] > 0, work, never, *operands)
+
+    def early_work(blocks, staged):
+        return answers_for(where, blocks, staged, narrow_size)
+
+    def shared_work(activations, across, shared_weight, maps):
+        pairs = {0: [activations] + ([across] if half else [])}
+        bit = half // 2
         while bit:
-            spread.update({j ^ bit: swap(x, "narrow", bit) for j, x in list(spread.items())})
+            for g, pair in list(pairs.items()):
+                pairs[g ^ bit] = [swap(x, "narrow", bit) for x in pair]
             bit //= 2
-        return base(where, [spread[j] for j in range(narrow_size)], shared_weight), stage(down_weight)
-
-    def never(activations, shared_weight, down_weight):
-        adapters, features, width = down_weight.shape
-        return jnp.zeros((rows, cols), f32), jnp.zeros((features, adapters * width), bf16)
-
-    base_out, staged = lax.cond(
-        begun[0, 0] > 0, beside_rows, never, activations, shared_weight, adapter_down_weight
-    )
-    ids, more, parts = low_rank_parts(
-        where, [after(b, base_out) for b in got], staged, cols, narrow_size
-    )
-    answers = raise_parts(ids, parts, up_weight, counts)
-    answers = [swap(answers[k], "wide", k) if k else answers[k] for k in range(wide_size)]
+        total = None
+        for g in sorted(pairs):
+            total = base(where, pairs[g], g, half, shared_weight, total)
+        return total, stage(*maps)
+
+    def late_work(blocks, staged):
+        outs, more = answers_for(where, blocks, staged, narrow_size)
+        return [swap(b, "wide", k) for k, b in zip(late, outs)], more
+
+    outs, more = step(early_work, [got[k] for k in early], staged)
+    more = more[0, 0]
+    answers = dict(zip(early, outs))
+    base_out, staged = step(
+        shared_work, *after_all((activations, across, shared_weight, maps), *outs)
+    )
+    if late:
+        arrived = [after(got[k], base_out) for k in late]
+        answers = {k: swap(after(b, *arrived), "wide", k) if k else b for k, b in answers.items()}
+        outs, flag = step(late_work, arrived, staged)
+        more = jnp.maximum(more, flag[0, 0])
+        answers.update(zip(late, outs))
+    else:
+        answers = {k: swap(b, "wide", k) if k else b for k, b in answers.items()}
+    answers = [answers[k] for k in range(wide_size)]
 
     def done(base_out):
         return join(base_out, place, answers, bf16)

time: 72 us -> 79.3 us (1.10)
  starting transfers between devices: 13.8 us -> 22.5 us
  waiting for transfers between devices: 34.3 us -> 26.9 us
  Pallas kernels: 19 us -> 26.2 us
  local copies, waits for them, and re-layouts: 3.21 us -> 1.19 us
  loops' own time: 0.07 us -> 1.39 us
    ppermute x12 -> x15, starting transfers between devices: 13.8 us -> 22.5 us  [swap(): return lax.ppermute(x, axis, [(i, i ^ k) for i in range(size)])]
    ppermute x12 -> x15, waiting for transfers between devices: 34.3 us -> 26.9 us  [swap(): return lax.ppermute(x, axis, [(i, i ^ k) for i in range(size)])]
    pallas_call x1 -> x2, Pallas kernels: 3.66 us -> 8.11 us  [stage(): pl.pallas_call(stage_kernel, out_shape=[pltpu.VMEM((features, adapters *...]
    pallas_call x1 -> x2, Pallas kernels: 4.78 us -> 6.96 us  [down(): pl.pallas_call(functools.partial(down_kernel, len(blocks), cols, narrow_s...]
    cond x4 -> x2, local copies, waits for them, and re-layouts: 2.5 us -> 1.16 us
    another operation x1 -> x3, loops' own time: 0.05 us -> 1.38 us  [step(): return lax.cond(begun[0, 0] > 0, work, never, *operands)]
    pallas_call x1 -> x2, Pallas kernels: 4.35 us -> 4.04 us  [base(): pl.pallas_call(functools.partial(base_kernel, count), grid_spec=pltpu.Pre...]
    pallas_call x1 -> x2, Pallas kernels: 1.88 us -> 1.58 us  [up(): pl.pallas_call(functools.partial(up_kernel, len(parts)), out_shape=[jax.S...]
  transfers between devices with their start and end apart: 12 -> 15, of which waited for: 4 -> 5; matrix products, arithmetic and copies ran while one was open for 0% -> 0% of each run, Pallas kernels for 11% -> 26%
where the time goes in v4:
time: 79.3 us; the launch traced here: 79 us
  waiting for transfers between devices  26.9 us (34%)
  Pallas kernels  26.2 us (33%)
  starting transfers between devices  22.5 us (28%)
  loops' own time  1.39 us (2%)
  local copies, waits for them, and re-layouts  1.19 us (2%)
  between operations  0.84 us (1%)
    ppermute x15, waiting for transfers between devices, swap(): return lax.ppermute(x, axis, [(i, i ^ k) for i in range(size)])  26.9 us
    ppermute x15, starting transfers between devices, swap(): return lax.ppermute(x, axis, [(i, i ^ k) for i in range(size)])  22.5 us
    pallas_call x2, Pallas kernels, stage(): pl.pallas_call(stage_kernel, out_shape=[pltpu.VMEM((features, adapters *...  8.11 us
    pallas_call x2, Pallas kernels, down(): pl.pallas_call(functools.partial(down_kernel, len(blocks), cols, narrow_s...  6.96 us
    pallas_call x2, Pallas kernels, base(): pl.pallas_call(functools.partial(base_kernel, count), grid_spec=pltpu.Pre...  4.04 us
    pallas_call x1, Pallas kernels, pack(): pl.pallas_call(functools.partial(pack_kernel, local_count, counts, before...  3.51 us
    pallas_call x1, Pallas kernels, join(): pl.pallas_call(join_kernel, out_shape=jax.ShapeDtypeStruct((rows, cols),...  1.95 us
  transfers between devices with their start and end apart: 15, of which 5 were waited for; matrix products, arithmetic and copies ran while one was open for 0% of the time, Pallas kernels for 26%

profile of v4, /device:TPU:0, one launch (start us, length us, event | category | flops | bytes accessed | tf_op | source)
XLA Modules:
  0.0 79.0 jit_solution(15798699775256122357)
XLA Ops:
  0.1 3.5 %pack_rows.6 = (s32[1,1]{1,0:T(1,128)}, f32[256,128]{1,0:T(8,128)}, bf16[112,2048]{1,0:T(8,128)(2,1)S(1)}, bf16[112,2048]{1,0:T(8,128)(2,1)S(1)}, bf16[96,2048]{...) custom-call(s32[3]{0:T(128)S(1)} %pad_add_fusion.1.where_ref, s32[1,256]{1,0:T(1,128)} %bitcast.19, s32[1,64]{1,0:T(1,128)} %bitcast.21, ...), custom_call_target="tpu_custom_call" | custom-call | flops 43620760 | bytes 275251 | tf_op jit(solution)/shard_map/pack_rows/pallas_call | solution.py:133
  3.6 3.0 %collective-permute-start.21 = (bf16[256,2048]{1,0:T(8,128)(2,1)}, bf16[256,2048]{1,0:T(8,128)(2,1)S(1)}, u32[]{:S(2)}, u32[]{:S(2)}) collective-permute-start(bf16[256,2048]{1,0:T(8,128)(2,1)} %act_ref.1), channel_id=1, source_target_pairs={{0,2},{1,3},{2,0},{3,1},{4,6},{5,7},{6,4},{7,5},{8,10},{9,11},{10,... | collective-permute-start | bytes 3145736 | tf_op jit(solution)/shard_map/ppermute | solution.py:30
  6.6 1.6 %collective-permute-start.19 = (bf16[112,2048]{1,0:T(8,128)(2,1)S(1)}, bf16[112,2048]{1,0:T(8,128)(2,1)S(1)}, u32[]{:S(2)}, u32[]{:S(2)}) collective-permute-start(bf16[112,2048]{1,0:T(8,128)(2,1)S(1)} %get-tuple-element.395), channel_id=1, source_target_pairs={{0,4},{4,0},{8,12},{12,8},{1,5},{5,1},{9,13},{13,9},{2,6},{6,2},{1... | collective-permute-start | bytes 1376264 | tf_op jit(solution)/shard_map/ppermute | solution.py:30
  8.2 2.5 %collective-permute-start.18 = (bf16[96,2048]{1,0:T(8,128)(2,1)S(1)}, bf16[96,2048]{1,0:T(8,128)(2,1)S(1)}, u32[]{:S(2)}, u32[]{:S(2)}) collective-permute-start(bf16[96,2048]{1,0:T(8,128)(2,1)S(1)} %get-tuple-element.394), channel_id=1, source_target_pairs={{0,12},{4,8},{8,4},{12,0},{1,13},{5,9},{9,5},{13,1},{2,14},{6,10},... | collective-permute-start | bytes 1179656 | tf_op jit(solution)/shard_map/ppermute | solution.py:30
  10.8 3.9 %stage_maps.7 = (bf16[2048,2048]{1,0:T(8,128)(2,1)S(1)}, bf16[1024,512]{1,0:T(8,128)(2,1)S(1)}) custom-call(bf16[16,2048,128]{2,1,0:T(8,128)(2,1)} %down_ref, bf16[1024,512]{1,0:T(8,128)(2,1)} %bitcast.9.up_ref), custom_call_target="tpu_custom_call" | custom-call | flops 1 | bytes 1 | tf_op jit(solution)/shard_map/stage_maps/pallas_call | solution.py:167
  15.4 15.2 %collective-permute-done.18 = bf16[96,2048]{1,0:T(8,128)(2,1)S(1)} collective-permute-done((bf16[96,2048]{1,0:T(8,128)(2,1)S(1)}, bf16[96,2048]{1,0:T(8,128)(2,1)S(1)}, u32[]{:S(2)}, u32[]{:S(2)}) %collective-permute-start.18) | collective-permute-done | bytes 393248 | tf_op jit(solution)/shard_map/ppermute | solution.py:30
  30.6 10.4 %conditional.4 = (bf16[96,512]{1,0:T(8,128)(2,1)}, bf16[112,512]{1,0:T(8,128)(2,1)}, bf16[112,512]{1,0:T(8,128)(2,1)}, s32[1,1]{1,0:T(1,128)}) conditional(s32[]{:T(128)} %bitcast.8, () %tuple.63, (s32[3]{0:T(128)S(1)}, bf16[96,2048]{1,0:T(8,128)(2,1)S(1)}, bf16[112,2048]{1,0:T(8,128)(2,1)S(1)}, bf16[112,2048]{1,0:T(8,128)(2,1)S(1)}, ...), branch_computations={%region_0.0_spmd, %region_1.0_spmd} | conditional | flops 301989888 | bytes 1631997 | solution.py:400
  30.6 3.9 %down_maps.7 = (s32[1,1]{1,0:T(1,128)}, f32[320,128]{1,0:T(8,128)S(1)}, f32[160,128]{1,0:T(8,128)S(1)}, bf16[160,128]{1,0:T(8,128)(2,1)S(1)}, bf16[160,128]{1,0:...) custom-call(s32[3]{0:T(128)S(1)} %get-tuple-element.285.where_ref, bf16[96,2048]{1,0:T(8,128)(2,1)S(1)} %get-tuple-element.286.refs_0_, ...), custom_call_target="tpu_custom_call" | custom-call | flops 268435456 | bytes 969932 | tf_op jit(solution)/shard_map/cond/branch_1_fun/down_maps/pallas_call | solution.py:229
  35.2 1.3 %collective-permute-start.2 = (bf16[160,128]{1,0:T(8,128)(2,1)S(1)}, bf16[160,128]{1,0:T(8,128)(2,1)S(1)}, u32[]{:S(2)}, u32[]{:S(2)}) collective-permute-start(bf16[160,128]{1,0:T(8,128)(2,1)S(1)} %get-tuple-element.294), channel_id=1, source_target_pairs={{0,3},{1,2},{2,1},{3,0},{4,7},{5,6},{6,5},{7,4},{8,11},{9,10},{10,... | collective-permute-start | bytes 122888 | tf_op jit(solution)/shard_map/cond/branch_1_fun/ppermute | solution.py:30
  36.5 2.6 %collective-permute-done.1.refs_2_ = bf16[160,128]{1,0:T(8,128)(2,1)S(1)} collective-permute-done((bf16[160,128]{1,0:T(8,128)(2,1)S(1)}, bf16[160,128]{1,0:T(8,128)(2,1)S(1)}, u32[]{:S(2)}, u32[]{:S(2)}) %collective-permute-start.1) | collective-permute-done | bytes 40992 | tf_op jit(solution)/shard_map/cond/branch_1_fun/ppermute | solution.py:30
  39.1 1.2 %up_maps.7 = (bf16[96,512]{1,0:T(8,128)(2,1)}, bf16[112,512]{1,0:T(8,128)(2,1)}, bf16[112,512]{1,0:T(8,128)(2,1)}) custom-call(f32[320,128]{1,0:T(8,128)S(1)} %get-tuple-element.290.ids_ref, f32[160,128]{1,0:T(8,128)S(1)} %get-tuple-element.291.refs_0_, bf16[160,128]{1,0:T(8,128)(2,1)S(1)} %collective-permute-done.refs_1_, ...), custom_call_target="tpu_custom_call" | custom-call | flops 33554432 | bytes 170393 | tf_op jit(solution)/shard_map/cond/branch_1_fun/up_maps/pallas_call | solution.py:274
  41.0 10.2 %conditional.5 = (f32[256,512]{1,0:T(8,128)S(1)}, bf16[2048,2048]{1,0:T(8,128)(2,1)S(1)}, bf16[1024,512]{1,0:T(8,128)(2,1)S(1)}) conditional(s32[]{:T(128)} %bitcast.8, () %tuple.67, (bf16[256,2048]{1,0:T(8,128)(2,1)S(1)}, bf16[256,2048]{1,0:T(8,128)(2,1)S(1)}, s32[3]{0:T(128)S(1)}, bf16[8192,512]{1,0:T(8,128)(2,1)}, ...), branch_computations={%region_2.0_spmd, %region_3.0_spmd} | conditional | flops 214748368 | bytes 43201460 | solution.py:400
  41.9 4.2 %stage_maps.5 = (bf16[2048,2048]{1,0:T(8,128)(2,1)S(1)}, bf16[1024,512]{1,0:T(8,128)(2,1)S(1)}) custom-call(bf16[16,2048,128]{2,1,0:T(8,128)(2,1)} %get-tuple-element.304.down_ref, bf16[1024,512]{1,0:T(8,128)(2,1)} %get-tuple-element.305.up_ref), custom_call_target="tpu_custom_call" | custom-call | flops 1 | bytes 1 | tf_op jit(solution)/shard_map/cond/branch_1_fun/stage_maps/pallas_call | solution.py:167
  47.2 2.0 %shared_projection.2.refs_3_ = f32[256,512]{1,0:T(8,128)S(1)} custom-call(s32[3]{0:T(128)S(1)} %get-tuple-element.300.where_ref, bf16[256,2048]{1,0:T(8,128)(2,1)S(1)} %get-tuple-element.301.refs_0_, bf16[256,2048]{1,0:T(8,128)(2,1)S(1)} %get-tuple-element.302.refs_1_, bf16[8192,512]{1,0:T(8,128)(2,1)S(1)} %copy-done.2), custom_call_target="tpu_custom_call" | custom-call | flops 107374184 | bytes 629145 | tf_op jit(solution)/shard_map/cond/branch_1_fun/shared_projection/pallas_call | solution.py:303
  49.2 2.0 %shared_projection.3 = f32[256,512]{1,0:T(8,128)S(1)} custom-call(s32[3]{0:T(128)S(1)} %get-tuple-element.300.where_ref, bf16[256,2048]{1,0:T(8,128)(2,1)S(1)} %collective-permute-done.3.refs_0_, bf16[256,2048]{1,0:T(8,128)(2,1)S(1)} %collective-permute-done.4.refs_1_, bf16[8192,512]{1,0:T(8,128)(2,1)S(1)} %copy-done.2, f32[256,512]{1,0:T(8,128)S(1)} %shared_projection.2.refs_3_), custom_call_target="tpu_custom_call" | custom-call | flops 107374184 | bytes 629145 | tf_op jit(solution)/shard_map/cond/branch_1_fun/shared_projection/pallas_call | solution.py:303
  51.3 7.7 %collective-permute-start.22 = (bf16[112,512]{1,0:T(8,128)(2,1)}, bf16[112,512]{1,0:T(8,128)(2,1)S(1)}, u32[]{:S(2)}, u32[]{:S(2)}) collective-permute-start(bf16[112,512]{1,0:T(8,128)(2,1)} %get-tuple-element.418), channel_id=1, source_target_pairs={{0,4},{4,0},{8,12},{12,8},{1,5},{5,1},{9,13},{13,9},{2,6},{6,2},{1... | collective-permute-start | bytes 344072 | tf_op jit(solution)/shard_map/ppermute | solution.py:30
  59.0 2.9 %collective-permute-start.23 = (bf16[96,512]{1,0:T(8,128)(2,1)}, bf16[96,512]{1,0:T(8,128)(2,1)S(1)}, u32[]{:S(2)}, u32[]{:S(2)}) collective-permute-start(bf16[96,512]{1,0:T(8,128)(2,1)} %get-tuple-element.420), channel_id=1, source_target_pairs={{0,12},{4,8},{8,4},{12,0},{1,13},{5,9},{9,5},{13,1},{2,14},{6,10},... | collective-permute-start | bytes 294920 | tf_op jit(solution)/shard_map/ppermute | solution.py:30
  61.9 15.1 %conditional.6 = (bf16[96,512]{1,0:T(8,128)(2,1)}, s32[1,1]{1,0:T(1,128)}) conditional(s32[]{:T(128)} %bitcast.8, () %tuple.66, (s32[3]{0:T(128)S(1)}, bf16[96,2048]{1,0:T(8,128)(2,1)}, bf16[2048,2048]{1,0:T(8,128)(2,1)S(1)}, bf16[1024,512]{1,0:T(8,128)(2,1)S(1)}) %tuple.72), branch_computations={%region_4.0_spmd, %region_5.0_spmd} | conditional | flops 90596968 | bytes 1543548 | solution.py:400
  61.9 3.0 %down_maps.8 = (s32[1,1]{1,0:T(1,128)}, f32[96,128]{1,0:T(8,128)S(1)}, f32[48,128]{1,0:T(8,128)S(1)}, bf16[48,128]{1,0:T(8,128)(2,1)S(1)}, bf16[48,128]{1,0:T(8,128)(2,1)S(1)}, /*index=5*/bf16[48,128]{1,0:T(8,128)(2,1)S(1)}) custom-call(s32[3]{0:T(128)S(1)} %get-tuple-element.308.where_ref, bf16[96,2048]{1,0:T(8,128)(2,1)} %get-tuple-element.309.refs_0_, ...), custom_call_target="tpu_custom_call" | custom-call | flops 80530640 | bytes 878182 | tf_op jit(solution)/shard_map/cond/branch_1_fun/down_maps/pallas_call | solution.py:229
  65.0 1.2 %collective-permute-start.6 = (bf16[48,128]{1,0:T(8,128)(2,1)S(1)}, bf16[48,128]{1,0:T(8,128)(2,1)S(1)}, u32[]{:S(2)}, u32[]{:S(2)}) collective-permute-start(bf16[48,128]{1,0:T(8,128)(2,1)S(1)} %get-tuple-element.314), channel_id=1, source_target_pairs={{0,2},{1,3},{2,0},{3,1},{4,6},{5,7},{6,4},{7,5},{8,10},{9,11},{10,... | collective-permute-start | bytes 36872 | tf_op jit(solution)/shard_map/cond/branch_1_fun/ppermute | solution.py:30
  66.9 1.9 %collective-permute-done.6.refs_2_ = bf16[48,128]{1,0:T(8,128)(2,1)S(1)} collective-permute-done((bf16[48,128]{1,0:T(8,128)(2,1)S(1)}, bf16[48,128]{1,0:T(8,128)(2,1)S(1)}, u32[]{:S(2)}, u32[]{:S(2)}) %collective-permute-start.6) | collective-permute-done | bytes 12320 | tf_op jit(solution)/shard_map/cond/branch_1_fun/ppermute | solution.py:30
  69.8 6.6 %collective-permute-done.8 = bf16[96,512]{1,0:T(8,128)(2,1)} collective-permute-done((bf16[96,512]{1,0:T(8,128)(2,1)S(1)}, bf16[96,512]{1,0:T(8,128)(2,1)}, u32[]{:S(2)}, u32[]{:S(2)}) %collective-permute-start.8) | collective-permute-done | bytes 98336 | tf_op jit(solution)/shard_map/cond/branch_1_fun/ppermute | solution.py:30
  77.1 2.0 %conditional.7 = (bf16[256,512]{1,0:T(8,128)(2,1)}) conditional(s32[]{:T(128)} %bitcast.10, (f32[256,512]{1,0:T(8,128)S(1)}, f32[256,128]{1,0:T(8,128)S(1)}, bf16[112,512]{1,0:T(8,128)(2,1)S(1)}, bf16[112,512]{1,0:T(8,128)(2,1)S(1)}, bf16[96,512]{1,0:T(8,128)(2,1)}, /*index=5*/bf16[96,512]{1,0:T(8,128)(2,1)S(1)}) %tuple.103, ...), branch_computations={%region_6.0_spmd, %region_7.0_spmd} | conditional | flops 148609424 | bytes 39928496 | solution.py:451
  77.1 1.9 %join_corrections.7 = bf16[256,512]{1,0:T(8,128)(2,1)} custom-call(f32[256,512]{1,0:T(8,128)S(1)} %get-tuple-element.318.base_ref, f32[256,128]{1,0:T(8,128)S(1)} %get-tuple-element.319.place_ref, bf16[112,512]{1,0:T(8,128)(2,1)S(1)} %get-tuple-element.320.refs_0_, bf16[112,512]{1,0:T(8,128)(2,1)S(1)} %get-tuple-element.321.refs_1_, ...), custom_call_target="tpu_custom_call" | custom-call | flops 10905190 | bytes 121241 | tf_op jit(solution)/shard_map/cond/branch_0_fun/join_corrections/pallas_call | solution.py:338
  (33 shorter events, 4.6 us)
Async XLA Ops:
  3.6 37.4 %collective-permute-start.21 = (bf16[256,2048]{1,0:T(8,128)(2,1)}, bf16[256,2048]{1,0:T(8,128)(2,1)S(1)}, u32[]{:S(2)}, u32[]{:S(2)}) collective-permute-start(bf16[256,2048]{1,0:T(8,128)(2,1)} %act_ref.1), channel_id=1, source_target_pairs={{0,2},{1,3},{2,0},{3,1},{4,6},{5,7},{6,4},{7,5},{8,10},{9,11},{10,... | collective-permute-start | bytes 3145736 | tf_op jit(solution)/shard_map/ppermute | solution.py:30
  6.6 24.0 %collective-permute-start.19 = (bf16[112,2048]{1,0:T(8,128)(2,1)S(1)}, bf16[112,2048]{1,0:T(8,128)(2,1)S(1)}, u32[]{:S(2)}, u32[]{:S(2)}) collective-permute-start(bf16[112,2048]{1,0:T(8,128)(2,1)S(1)} %get-tuple-element.395), channel_id=1, source_target_pairs={{0,4},{4,0},{8,12},{12,8},{1,5},{5,1},{9,13},{13,9},{2,6},{6,2},{1... | collective-permute-start | bytes 1376264 | tf_op jit(solution)/shard_map/ppermute | solution.py:30
  8.2 22.4 %collective-permute-start.18 = (bf16[96,2048]{1,0:T(8,128)(2,1)S(1)}, bf16[96,2048]{1,0:T(8,128)(2,1)S(1)}, u32[]{:S(2)}, u32[]{:S(2)}) collective-permute-start(bf16[96,2048]{1,0:T(8,128)(2,1)S(1)} %get-tuple-element.394), channel_id=1, source_target_pairs={{0,12},{4,8},{8,4},{12,0},{1,13},{5,9},{9,5},{13,1},{2,14},{6,10},... | collective-permute-start | bytes 1179656 | tf_op jit(solution)/shard_map/ppermute | solution.py:30
  10.7 40.7 %collective-permute-start.20 = (bf16[96,2048]{1,0:T(8,128)(2,1)S(1)}, bf16[96,2048]{1,0:T(8,128)(2,1)}, u32[]{:S(2)}, u32[]{:S(2)}) collective-permute-start(bf16[96,2048]{1,0:T(8,128)(2,1)S(1)} %get-tuple-element.397), channel_id=1, source_target_pairs={{0,8},{4,12},{8,0},{12,4},{1,9},{5,13},{9,1},{13,5},{2,10},{6,14},... | collective-permute-start | bytes 1179656 | tf_op jit(solution)/shard_map/ppermute | solution.py:30
  10.8 30.2 %copy-start.1 = (bf16[256,2048]{1,0:T(8,128)(2,1)S(1)}, bf16[256,2048]{1,0:T(8,128)(2,1)}, u32[]{:S(2)}) copy-start(bf16[256,2048]{1,0:T(8,128)(2,1)} %act_ref.1) | copy-start | bytes 3145732
  34.6 1.9 %collective-permute-start = (bf16[160,128]{1,0:T(8,128)(2,1)S(1)}, bf16[160,128]{1,0:T(8,128)(2,1)S(1)}, u32[]{:S(2)}, u32[]{:S(2)}) collective-permute-start(bf16[160,128]{1,0:T(8,128)(2,1)S(1)} %get-tuple-element.292), channel_id=1, source_target_pairs={{0,1},{1,0},{2,3},{3,2},{4,5},{5,4},{6,7},{7,6},{8,9},{9,8},{10,11... | collective-permute-start | bytes 122888 | tf_op jit(solution)/shard_map/cond/branch_1_fun/ppermute | solution.py:30
  34.6 4.5 %collective-permute-start.1 = (bf16[160,128]{1,0:T(8,128)(2,1)S(1)}, bf16[160,128]{1,0:T(8,128)(2,1)S(1)}, u32[]{:S(2)}, u32[]{:S(2)}) collective-permute-start(bf16[160,128]{1,0:T(8,128)(2,1)S(1)} %get-tuple-element.293), channel_id=1, source_target_pairs={{0,2},{1,3},{2,0},{3,1},{4,6},{5,7},{6,4},{7,5},{8,10},{9,11},{10,... | collective-permute-start | bytes 122888 | tf_op jit(solution)/shard_map/cond/branch_1_fun/ppermute | solution.py:30
  35.2 3.9 %collective-permute-start.2 = (bf16[160,128]{1,0:T(8,128)(2,1)S(1)}, bf16[160,128]{1,0:T(8,128)(2,1)S(1)}, u32[]{:S(2)}, u32[]{:S(2)}) collective-permute-start(bf16[160,128]{1,0:T(8,128)(2,1)S(1)} %get-tuple-element.294), channel_id=1, source_target_pairs={{0,3},{1,2},{2,1},{3,0},{4,7},{5,6},{6,5},{7,4},{8,11},{9,10},{10,... | collective-permute-start | bytes 122888 | tf_op jit(solution)/shard_map/cond/branch_1_fun/ppermute | solution.py:30
  41.0 6.2 %copy-start.2 = (bf16[8192,512]{1,0:T(8,128)(2,1)S(1)}, bf16[8192,512]{1,0:T(8,128)(2,1)}, u32[]{:S(2)}) copy-start(bf16[8192,512]{1,0:T(8,128)(2,1)} %get-tuple-element.303.refs_2_) | copy-start | bytes 25165828 | tf_op jit(solution)/shard_map/cond
  41.0 8.2 %collective-permute-start.3 = (bf16[256,2048]{1,0:T(8,128)(2,1)S(1)}, bf16[256,2048]{1,0:T(8,128)(2,1)S(1)}, u32[]{:S(2)}, u32[]{:S(2)}) collective-permute-start(bf16[256,2048]{1,0:T(8,128)(2,1)S(1)} %get-tuple-element.301.refs_0_), channel_id=1, source_target_pairs={{0,1},{1,0},{2,3},{3,2},{4,5},{5,4},{6,7},{7,6},{8,9},{9,8},{10,11... | collective-permute-start | bytes 3145736 | tf_op jit(solution)/shard_map/cond/branch_1_fun/ppermute | solution.py:30
  41.8 7.5 %collective-permute-start.4 = (bf16[256,2048]{1,0:T(8,128)(2,1)S(1)}, bf16[256,2048]{1,0:T(8,128)(2,1)S(1)}, u32[]{:S(2)}, u32[]{:S(2)}) collective-permute-start(bf16[256,2048]{1,0:T(8,128)(2,1)S(1)} %get-tuple-element.302.refs_1_), channel_id=1, source_target_pairs={{0,1},{1,0},{2,3},{3,2},{4,5},{5,4},{6,7},{7,6},{8,9},{9,8},{10,11... | collective-permute-start | bytes 3145736 | tf_op jit(solution)/shard_map/cond/branch_1_fun/ppermute | solution.py:30
  51.3 25.8 %copy-start.3 = (bf16[112,512]{1,0:T(8,128)(2,1)S(1)}, bf16[112,512]{1,0:T(8,128)(2,1)}, u32[]{:S(2)}) copy-start(bf16[112,512]{1,0:T(8,128)(2,1)} %get-tuple-element.406) | copy-start | bytes 344068
  51.3 25.8 %copy-start.5 = (f32[256,128]{1,0:T(8,128)S(1)}, f32[256,128]{1,0:T(8,128)}, u32[]{:S(2)}) copy-start(f32[256,128]{1,0:T(8,128)} %get-tuple-element.417) | copy-start | bytes 393220
  51.3 25.8 %copy-start.7 = (s32[256,1]{0,1:T(1,128)S(1)}, s32[256,1]{0,1:T(1,128)}, u32[]{:S(2)}) copy-start(s32[256,1]{0,1:T(1,128)} %param.17) | copy-start | bytes 3076
  51.3 25.8 %copy-start.8 = (s32[64]{0:T(128)S(1)}, s32[64]{0:T(128)}, u32[]{:S(2)}) copy-start(s32[64]{0:T(128)} %param.18) | copy-start | bytes 772
  51.3 25.7 %collective-permute-start.22 = (bf16[112,512]{1,0:T(8,128)(2,1)}, bf16[112,512]{1,0:T(8,128)(2,1)S(1)}, u32[]{:S(2)}, u32[]{:S(2)}) collective-permute-start(bf16[112,512]{1,0:T(8,128)(2,1)} %get-tuple-element.418), channel_id=1, source_target_pairs={{0,4},{4,0},{8,12},{12,8},{1,5},{5,1},{9,13},{13,9},{2,6},{6,2},{1... | collective-permute-start | bytes 344072 | tf_op jit(solution)/shard_map/ppermute | solution.py:30
  59.0 18.0 %collective-permute-start.23 = (bf16[96,512]{1,0:T(8,128)(2,1)}, bf16[96,512]{1,0:T(8,128)(2,1)S(1)}, u32[]{:S(2)}, u32[]{:S(2)}) collective-permute-start(bf16[96,512]{1,0:T(8,128)(2,1)} %get-tuple-element.420), channel_id=1, source_target_pairs={{0,12},{4,8},{8,4},{12,0},{1,13},{5,9},{9,5},{13,1},{2,14},{6,10},... | collective-permute-start | bytes 294920 | tf_op jit(solution)/shard_map/ppermute | solution.py:30
  64.9 1.9 %collective-permute-start.5 = (bf16[48,128]{1,0:T(8,128)(2,1)S(1)}, bf16[48,128]{1,0:T(8,128)(2,1)S(1)}, u32[]{:S(2)}, u32[]{:S(2)}) collective-permute-start(bf16[48,128]{1,0:T(8,128)(2,1)S(1)} %get-tuple-element.313), channel_id=1, source_target_pairs={{0,1},{1,0},{2,3},{3,2},{4,5},{5,4},{6,7},{7,6},{8,9},{9,8},{10,11... | collective-permute-start | bytes 36872 | tf_op jit(solution)/shard_map/cond/branch_1_fun/ppermute | solution.py:30
  65.0 3.8 %collective-permute-start.6 = (bf16[48,128]{1,0:T(8,128)(2,1)S(1)}, bf16[48,128]{1,0:T(8,128)(2,1)S(1)}, u32[]{:S(2)}, u32[]{:S(2)}) collective-permute-start(bf16[48,128]{1,0:T(8,128)(2,1)S(1)} %get-tuple-element.314), channel_id=1, source_target_pairs={{0,2},{1,3},{2,0},{3,1},{4,6},{5,7},{6,4},{7,5},{8,10},{9,11},{10,... | collective-permute-start | bytes 36872 | tf_op jit(solution)/shard_map/cond/branch_1_fun/ppermute | solution.py:30
  66.2 3.1 %collective-permute-start.7 = (bf16[48,128]{1,0:T(8,128)(2,1)S(1)}, bf16[48,128]{1,0:T(8,128)(2,1)S(1)}, u32[]{:S(2)}, u32[]{:S(2)}) collective-permute-start(bf16[48,128]{1,0:T(8,128)(2,1)S(1)} %get-tuple-element.315), channel_id=1, source_target_pairs={{0,3},{1,2},{2,1},{3,0},{4,7},{5,6},{6,5},{7,4},{8,11},{9,10},{10,... | collective-permute-start | bytes 36872 | tf_op jit(solution)/shard_map/cond/branch_1_fun/ppermute | solution.py:30
  69.7 6.7 %collective-permute-start.8 = (bf16[96,512]{1,0:T(8,128)(2,1)S(1)}, bf16[96,512]{1,0:T(8,128)(2,1)}, u32[]{:S(2)}, u32[]{:S(2)}) collective-permute-start(bf16[96,512]{1,0:T(8,128)(2,1)S(1)} %up_maps.8), channel_id=1, source_target_pairs={{0,8},{4,12},{8,0},{12,4},{1,9},{5,13},{9,1},{13,5},{2,10},{6,14},... | collective-permute-start | bytes 294920 | tf_op jit(solution)/shard_map/cond/branch_1_fun/ppermute | solution.py:30
